TPU v7x, 128 devices: a whole 4x4x4 slice. The times are simulated.
128 devices in a mesh: dp: 2 (over x_hi), dap: 64 (over z, y, x_lo, core).
Axes of the slice: x: 4 (x_hi: 2, x_lo: 2; x = x_hi * 2 + x_lo), y: 4, z: 4, core: 2. Of those that a mesh axis runs over, the one named last changes fastest.
Arguments:
- pair: bfloat16 [768, 384, 128], P(('dp', 'dap')), parts along dimension 0, may hold values from -6 to 6
- grad_out: bfloat16 [768, 384, 128], P(('dp', 'dap')), parts along dimension 0, may hold values from -16 to 16
- pad_mask: int32 [768], P('dp'), parts along dimension 0, may hold values 0 or 1
- chain_ids: int32 [768], P('dp'), parts along dimension 0, may hold values from 0 to 3, never falling along the last dimension, each value on 1 to 192 neighbouring positions
- chain_bias: float32 [128], replicated, may hold values from -6 to 6
- w_in: bfloat16 [128, 512], replicated, may hold values from -0.5 to 0.5
- w_gate: bfloat16 [128, 128], replicated, may hold values from -0.5 to 0.5
- w_out: bfloat16 [128, 128], replicated, may hold values from -0.5 to 0.5
Outputs:
- update: bfloat16 [768, 384, 128], P(('dp', 'dap')), parts along dimension 0
- grad_pair: bfloat16 [768, 384, 128], P(('dp', 'dap')), parts along dimension 0
- grad_w_in: float32 [256, 512], P('dp'), parts along dimension 0
- grad_w_gate: float32 [256, 128], P('dp'), parts along dimension 0
- grad_w_out: float32 [256, 128], P('dp'), parts along dimension 0
- grad_chain_bias: float32 [256], P('dp'), parts along dimension 0
There are 2 independent parts, one for each index of `dp`. A program takes and returns all parts, laid end to end along the dimension named above; an argument that names none is the same for every part. Nothing has to cross between parts.
Inputs may be any that keep to these rules, and one draw needn't show every extreme that they name: `chain_ids`: chain numbers never fall along the residues.
All inputs are finite; a program needn't handle non-finite values.
Results may differ from a plain program's by a relative error of at most 0.0081.
Values may be sent and summed in bfloat16 or wider, within the bound.
A program may use at most 384 MiB of HBM per device.

v0:
```python
import jax
import jax.numpy as jnp
from jax import lax
from jax.sharding import PartitionSpec as P

epsilon = 1e-05


def normalize(values):
    center = values - jnp.mean(values, axis=-1, keepdims=True)
    inverse = lax.rsqrt(jnp.mean(center * center, axis=-1, keepdims=True) + epsilon)
    return (center * inverse, inverse)


def norm_back(grad_norm, normed, inverse):
    first = jnp.mean(grad_norm, axis=-1, keepdims=True)
    second = jnp.mean(grad_norm * normed, axis=-1, keepdims=True)
    return inverse * (grad_norm - first - normed * second)


def on_device(pair, grad_out, pad_mask, chain_ids, chain_bias, w_in, w_gate, w_out):
    own_rows = pair.shape[0]
    residues = pair.shape[1]
    channels = pair.shape[2]
    hidden = w_out.shape[0]
    row_start = lax.axis_index("dap") * own_rows
    own_chain = lax.dynamic_slice_in_dim(chain_ids, row_start, own_rows)
    own_pad = lax.dynamic_slice_in_dim(pad_mask, row_start, own_rows)
    same_chain = (own_chain[:, None] == chain_ids[None, :]).astype(jnp.float32)[:, :, None]
    pair_mask = (own_pad.astype(jnp.float32)[:, None] * pad_mask.astype(jnp.float32)[None, :])[
        :, :, None
    ]
    z_input = pair.astype(jnp.float32) + same_chain * chain_bias
    z_hat, z_inverse = normalize(z_input)
    z_norm = z_hat.astype(jnp.bfloat16)
    cells = own_rows * residues
    z_flat = z_norm.reshape(cells, channels)
    projected = jnp.dot(z_flat, w_in, preferred_element_type=jnp.float32).reshape(
        own_rows, residues, 4 * hidden
    )
    gate_a = projected[:, :, :hidden]
    proj_a = projected[:, :, hidden : 2 * hidden]
    gate_b = projected[:, :, 2 * hidden : 3 * hidden]
    proj_b = projected[:, :, 3 * hidden :]
    sig_a = jax.nn.sigmoid(gate_a)
    sig_b = jax.nn.sigmoid(gate_b)
    left_a = (sig_a * proj_a * pair_mask).astype(jnp.bfloat16)
    right_b = (sig_b * proj_b * pair_mask).astype(jnp.bfloat16)
    right_all = lax.all_gather(right_b, "dap", axis=0, tiled=True)
    mixed = jnp.einsum("ikc,jkc->ijc", left_a, right_all, preferred_element_type=jnp.float32)
    x_hat, x_inverse = normalize(mixed)
    x_norm = x_hat.astype(jnp.bfloat16)
    x_flat = x_norm.reshape(cells, hidden)
    gate_logit = jnp.dot(z_flat, w_gate, preferred_element_type=jnp.float32)
    gate_value = jax.nn.sigmoid(gate_logit)
    out_lin = jnp.dot(x_flat, w_out, preferred_element_type=jnp.float32)
    update = (gate_value * out_lin).astype(jnp.bfloat16).reshape(own_rows, residues, channels)
    cotangent = grad_out.astype(jnp.float32).reshape(cells, channels)
    grad_u = (cotangent * gate_value).astype(jnp.bfloat16)
    grad_s = (cotangent * out_lin * gate_value * (1.0 - gate_value)).astype(jnp.bfloat16)
    local_w_out = jnp.dot(x_flat.T, grad_u, preferred_element_type=jnp.float32)
    local_w_gate = jnp.dot(z_flat.T, grad_s, preferred_element_type=jnp.float32)
    grad_xn = jnp.dot(grad_u, w_out.T, preferred_element_type=jnp.float32).reshape(
        own_rows, residues, hidden
    )
    grad_mixed = norm_back(grad_xn, x_hat, x_inverse).astype(jnp.bfloat16)
    grad_left = jnp.einsum(
        "ijc,jkc->ikc", grad_mixed, right_all, preferred_element_type=jnp.float32
    )
    mixed_cols = lax.all_to_all(grad_mixed, "dap", split_axis=1, concat_axis=0, tiled=True)
    grad_right = jnp.einsum(
        "ijc,ikc->jkc",
        mixed_cols,
        lax.all_gather(left_a, "dap", axis=0, tiled=True),
        preferred_element_type=jnp.float32,
    )
    grad_proj = (
        jnp.concatenate(
            [
                grad_left * proj_a * pair_mask * sig_a * (1.0 - sig_a),
                grad_left * sig_a * pair_mask,
                grad_right * proj_b * pair_mask * sig_b * (1.0 - sig_b),
                grad_right * sig_b * pair_mask,
            ],
            axis=-1,
        )
        .astype(jnp.bfloat16)
        .reshape(cells, 4 * hidden)
    )
    local_w_in = jnp.dot(z_flat.T, grad_proj, preferred_element_type=jnp.float32)
    grad_zn = jnp.dot(grad_proj, w_in.T, preferred_element_type=jnp.float32)
    grad_zn = grad_zn + jnp.dot(grad_s, w_gate.T, preferred_element_type=jnp.float32)
    grad_input = norm_back(grad_zn.reshape(own_rows, residues, channels), z_hat, z_inverse)
    local_chain = jnp.sum(same_chain * grad_input, axis=(0, 1))
    grad_pair = grad_input.astype(jnp.bfloat16)
    summed_in, summed_gate, summed_out, summed_chain = lax.psum(
        (local_w_in, local_w_gate, local_w_out, local_chain), "dap"
    )
    return (
        update,
        grad_pair,
        summed_in / residues,
        summed_gate / residues,
        summed_out / residues,
        summed_chain / residues,
    )


def solution(mesh):
    placed = (
        P(("dp", "dap"), None, None),
        P(("dp", "dap"), None, None),
        P("dp"),
        P("dp"),
        P(),
        P(),
        P(),
        P(),
    )
    return jax.shard_map(
        on_device,
        mesh=mesh,
        in_specs=placed,
        out_specs=(
            P(("dp", "dap"), None, None),
            P(("dp", "dap"), None, None),
            P("dp", None),
            P("dp", None),
            P("dp", None),
            P("dp"),
        ),
        check_vma=False,
    )
```

profile of v0, /device:TPU:1, one launch (start us, length us, event | category | flops | bytes accessed | tf_op | source)
XLA Modules:
  0.0 1062.6 jit_solution(9458558698708944501)
XLA Ops:
  7.2 0.0 copy-start
  7.2 0.0 all-gather.3.cloned.1.call-start
  7.3 0.7 convert_element_type.50
  8.0 0.8 dynamic-slice_convert_fusion
  8.8 0.8 dynamic_slice.6
  9.5 0.8 compare_convert_fusion
  10.3 1.8 fusion.44
  12.0 2.1 multiply_reduce_fusion.4
  14.2 1.2 fusion.46
  15.4 0.8 fusion.51
  16.1 0.1 broadcast_multiply_fusion.5
  16.2 2.1 multiply_convert_fusion.2
  18.3 0.3 copy-done.1
  18.7 0.0 all-gather.3.cloned.1.call-update
  18.7 0.0 all-gather.5.cloned.1.call-start
  18.7 0.7 all-gather.5.cloned.1.call-update
  19.4 0.3 copy-done.4
  19.7 1.4 copy.51
  21.1 210.4 %all-gather.3.cloned.1.call-done = bf16[384,384,128]{2,1,0:T(8,128)(2,1)} async-done(((bf16[6,384,128]{2,1,0:T(8,128)(2,1)}), bf16[384,384,128]{2,1,0:T(8,128)(2,1)}) %all-gather.3.cloned.1.call-update) | async-done | bytes 37748752 | tf_op jit(solution)/shard_map/all_gather | solution.py:49
  231.5 47.9 %copy.50 = bf16[384,384,128]{1,0,2:T(8,128)(2,1)} copy(bf16[384,384,128]{2,1,0:T(8,128)(2,1)} %all-gather.3.cloned.1.call-done) | data formatting | bytes 75497472 | tf_op jit(solution)/shard_map/all_gather | solution.py:49
  279.4 18.6 %bitcast_reduce_fusion = (f32[6,384]{1,0:T(8,128)S(1)}, f32[128,384,6]{1,2,0:T(8,128)S(1)}) fusion(bf16[384,384,128]{1,0,2:T(8,128)(2,1)} %copy.50, bf16[6,384,128]{1,0,2:T(8,128)(2,1)} %copy.51), kind=kOutput, calls=%fused_computation.22 | convolution fusion | flops 226785024 | bytes 39527424 | tf_op jit(solution)/shard_map/ikc,jkc->ijc/dot_general | solution.py:50
  298.1 0.3 multiply_reduce_fusion.1
  298.4 1.1 fusion.20
  299.5 1.6 copy.52
  301.1 1.2 fusion.57
  302.3 0.1 copy-done.18
  302.4 1.8 fusion.24
  304.2 0.8 copy-done.9
  305.1 1.2 fusion.55
  306.2 1.7 copy.53
  307.9 0.7 broadcast_multiply_fusion.4
  308.6 1.9 multiply_reduce_fusion
  310.5 0.1 copy-done.3
  310.6 0.4 multiply_convert_fusion
  311.0 1.6 copy.57
  312.5 8.3 all-to-all-start
  320.8 0.2 all-reduce.3.cloned.1.call-start
  321.0 14.2 %fusion.58 = f32[128,384,6]{1,2,0:T(8,128)S(1)} fusion(bf16[384,384,128]{1,0,2:T(8,128)(2,1)} %copy.50, bf16[6,384,128]{1,0,2:T(8,128)(2,1)S(1)} %multiply_convert_fusion), kind=kOutput, calls=%fused_computation.94 | convolution fusion | flops 226492416 | bytes 39518208 | tf_op jit(solution)/shard_map/ijc,jkc->ikc/dot_general | solution.py:67
  335.3 1.5 copy.56
  336.8 115.4 %all-gather.5.cloned.1.call-done = bf16[384,384,128]{2,1,0:T(8,128)(2,1)} async-done(((bf16[6,384,128]{2,1,0:T(8,128)(2,1)}), bf16[384,384,128]{2,1,0:T(8,128)(2,1)}) %all-gather.5.cloned.1.call-update) | async-done | bytes 37748752 | tf_op jit(solution)/shard_map/all_gather | solution.py:74
  452.2 47.3 %copy.60 = bf16[384,384,128]{1,0,2:T(8,128)(2,1)} copy(bf16[384,384,128]{2,1,0:T(8,128)(2,1)} %all-gather.5.cloned.1.call-done) | data formatting | bytes 75497472 | tf_op jit(solution)/shard_map/all_gather | solution.py:74
  499.5 1.0 fusion.61
  500.5 0.1 copy-done.8
  500.6 0.2 copy-done.11
  500.8 1.0 fusion.60
  501.8 1.3 copy.59
  503.0 0.2 all_to_all.16
  503.3 1.3 copy.61
  504.6 14.5 %fusion.59 = f32[128,384,6]{1,2,0:T(8,128)S(1)} fusion(bf16[384,384,128]{1,0,2:T(8,128)(2,1)} %copy.60, bf16[384,6,128]{0,1,2:T(8,128)(2,1)} %copy.61), kind=kOutput, calls=%fused_computation.95 | convolution fusion | flops 226492416 | bytes 39518208 | tf_op jit(solution)/shard_map/ijc,ikc->jkc/dot_general | solution.py:71
  519.1 1.5 copy.62
  520.6 3.7 fusion.40
  524.3 0.8 copy-done.12
  525.1 0.2 copy-done.13
  525.3 1.2 fusion.47
  526.5 2.0 fusion.3
  528.6 0.5 fusion.56
  529.1 1.5 multiply_reduce_fusion.3
  530.7 0.0 all-reduce.3.cloned.1.call-update
  530.7 2.7 multiply_reduce_fusion.2
  533.4 138.1 %psum.31 = f32[128]{0:T(128)S(1)} all-reduce(f32[128]{0:T(128)S(1)} %get-tuple-element.19), channel_id=1, replica_groups=mesh['dp'=2,'dap'=64] {'dap'}, use_global_device_ids=true, to_apply=%region_12.0 | all-reduce | flops 128 | bytes 1024 | tf_op jit(solution)/shard_map/psum | solution.py:96
  671.5 0.5 broadcast_multiply_fusion.10
  672.0 380.9 %all-reduce.3.cloned.1.call-done = (f32[128,512]{1,0:T(8,128)}, f32[128,128]{1,0:T(8,128)}, f32[128,128]{1,0:T(8,128)}) async-done(((f32[128,512]{1,0:T(8,128)}, f32[128,128]{1,0:T(8,128)}, f32[128,128]{1,0:T(8,128)}), (f32[128,512]{1,0:T(8,128)}, f32[128,128]{1,0:T(8,128)}, f32[128,128]{1,0:T(8,128)})) %all-reduce.3.cloned.1.call-update) | async-done | bytes 393232 | tf_op jit(solution)/shard_map/psum | solution.py:96
  1052.9 1.7 broadcast_multiply_fusion
  1054.6 1.5 broadcast_multiply_fusion.1
  (38 shorter events, 0.1 us)
Async XLA Ops:
  7.2 8.2 copy-start
  7.2 7.0 copy-start.2
  7.2 7.0 copy-start.17
  7.2 224.3 %all-gather.3.cloned.1.call-start = ((), (), s32[]{:S(2)}) async-start(), calls=%async_computation.1 | async-start | bytes 38338560 | tf_op jit(solution)/shard_map/all_gather | solution.py:49
  15.4 286.9 %copy-start.7 = (bf16[6,384,128]{2,1,0:T(8,128)(2,1)}, bf16[6,384,128]{2,1,0:T(8,128)(2,1)S(1)}, u32[]{:S(2)}) copy-start(bf16[6,384,128]{2,1,0:T(8,128)(2,1)S(1)} %fusion.46) | copy-start | bytes 1769476
  16.1 2.5 copy-start.1
  18.6 1.1 copy-start.4
  18.7 433.5 %all-gather.5.cloned.1.call-start = ((), (), s32[]{:S(2)}) async-start(), calls=%async_computation.2 | async-start | bytes 38338560 | tf_op jit(solution)/shard_map/all_gather | solution.py:74
  301.1 3.2 copy-start.5
  301.1 1.2 copy-start.15
  301.1 1.3 copy-start.18
  302.4 2.7 copy-start.14
  304.2 0.8 copy-start.9
  308.6 2.0 copy-start.3
  312.5 189.2 %all-to-all-start = ((bf16[6,384,128]{2,0,1:T(8,128)(2,1)}), bf16[6,384,128]{2,0,1:T(8,128)(2,1)}, u32[]{:S(2)}, u32[]{:S(2)}) async-start(bf16[6,384,128]{2,0,1:T(8,128)(2,1)} %copy.57), calls=%async_computation | async-start | bytes 1572864 | tf_op jit(solution)/shard_map/all_to_all | solution.py:70
  320.8 732.1 %all-reduce.3.cloned.1.call-start = ((), (), s32[]{:S(2)}) async-start(), calls=%async_computation.3 | async-start | bytes 786432 | tf_op jit(solution)/shard_map/psum | solution.py:96
  336.8 162.7 %copy-start.6 = (bf16[6,384,128]{2,1,0:T(8,128)(2,1)S(1)}, bf16[6,384,128]{2,1,0:T(8,128)(2,1)}, u32[]{:S(2)}) copy-start(bf16[6,384,128]{2,1,0:T(8,128)(2,1)} %copy-done.5) | copy-start | bytes 1769476
  336.8 162.7 %copy-start.10 = (bf16[2304,128]{1,0:T(8,128)(2,1)S(1)}, bf16[2304,128]{1,0:T(8,128)(2,1)}, u32[]{:S(2)}) copy-start(bf16[2304,128]{1,0:T(8,128)(2,1)} %copy-done.9) | copy-start | bytes 1769476
  499.5 1.1 copy-start.8
  499.5 1.2 copy-start.11
  524.3 0.8 copy-start.12
  524.3 1.0 copy-start.13
  526.5 2.0 copy-start.16
Sparse Core Ops, SparseCore 0:
  18.8 212.6 all-gather.2
  233.8 218.3 all-gather.4
  530.8 522.0 all-reduce.2
where the time goes:
time: 1070 us; the launch traced here: 1060 us
  waiting for transfers between devices  707 us (66%)
  blocking collectives  138 us (13%)
  local copies, waits for them, and re-layouts  111 us (10%)
  matrix products  58 us (5%)
  other arithmetic  25.5 us (2%)
  between operations  14 us (1%)
    psum x1, waiting for transfers between devices, on_device(): lax.psum((local_w_in, local_w_gate, local_w_out, local_chain), 'dap')  381 us
    all_gather x1, waiting for transfers between devices, on_device(): right_all = lax.all_gather(right_b, 'dap', axis=0, tiled=True)  210 us
    psum x1, blocking collectives, on_device(): lax.psum((local_w_in, local_w_gate, local_w_out, local_chain), 'dap')  138 us
    all_gather x1, waiting for transfers between devices, on_device(): lax.all_gather(left_a, 'dap', axis=0, tiled=True)  115 us
    all_gather x1, local copies, waits for them, and re-layouts, on_device(): right_all = lax.all_gather(right_b, 'dap', axis=0, tiled=True)  47.9 us
    all_gather x1, local copies, waits for them, and re-layouts, on_device(): lax.all_gather(left_a, 'dap', axis=0, tiled=True)  47.3 us
  transfers between devices with their start and end apart: 4, of which 3 were waited for; matrix products, arithmetic and copies ran while one was open for 14% of the time, Pallas kernels for 0%

commit v1 on v0

v1 whole, which is shorter than its diff:
```python
import functools

import jax
import jax.numpy as jnp
from jax import lax
from jax.experimental import pallas as pl
from jax.experimental.pallas import tpu as pltpu
from jax.sharding import PartitionSpec as P

epsilon = 1e-05
f32 = jnp.float32
bf16 = jnp.bfloat16

RING = 4
PAIR = 2
B, A, X, DX, DA, DB = range(6)


def nn(left, right):
    return jnp.dot(left, right, preferred_element_type=f32)


def nt(left, right):
    return lax.dot_general(left, right, (((1,), (1,)), ((), ())), preferred_element_type=f32)


def sigmoid(values):
    return 0.5 * jnp.tanh(0.5 * values) + 0.5


def mean0(values):
    return jnp.mean(values, axis=0, keepdims=True)


def kernel(
    planes,
    pair, gout, pad_v, chain_v, pad_s, chain_s, bias, w_in, w_gate, w_out,
    update, gpair, gw_in, gw_gate, gw_out, gw_chain,
    s_snd, s_rcv, r_snd, r_rcv,
    z, rz, sig_a, lin_a, sig_b, lin_b, gate, gout_t, du, dxn, xn, ds,
    bias_t, wt_in, wt_gate, wt_out, gather, scatter, order, order_t, bn, dxt,
    g_sum, g_rcv, h_snd, h_rcv, o_snd, o_rcv, chain_sum,
    s_ssem, s_rsem, r_ssem, r_rsem, g_ssem, g_rsem,
):
    rows, n, channels = pair.shape
    chunks = rows // PAIR
    lanes = n // chunks
    per_plane = channels // planes
    mine = per_plane // RING
    part = planes * PAIR
    me = lax.axis_index("dap")
    plane = lax.div(me, RING)
    place = lax.rem(me, RING)

    def at_plane(k):
        return lax.rem(plane + k, planes)

    def at_place(k):
        return lax.rem(place + k, RING)

    barrier = pltpu.get_barrier_semaphore()

    @pl.loop(1, planes)
    def _(k):
        pl.semaphore_signal(barrier, inc=1, device_id={"dap": at_plane(k) * RING + place}, device_id_type=pl.DeviceIdType.MESH)

    @pl.loop(1, RING)
    def _(k):
        pl.semaphore_signal(barrier, inc=1, device_id={"dap": plane * RING + at_place(k)}, device_id_type=pl.DeviceIdType.MESH)

    def send_planes(src, dst, ssem, rsem):
        @pl.loop(1, planes)
        def _(k):
            to = at_plane(k)
            pltpu.make_async_remote_copy(
                src_ref=src(to), dst_ref=dst(plane), send_sem=ssem, recv_sem=rsem,
                device_id={"dap": to * RING + place}, device_id_type=pl.DeviceIdType.MESH,
            ).start()

    def send_places(src, dst, ssem, rsem):
        @pl.loop(1, RING)
        def _(k):
            to = at_place(k)
            pltpu.make_async_remote_copy(
                src_ref=src(to), dst_ref=dst(place), send_sem=ssem, recv_sem=rsem,
                device_id={"dap": plane * RING + to}, device_id_type=pl.DeviceIdType.MESH,
            ).start()

    def wait(ref, sem):
        pltpu.make_async_copy(ref, ref, sem).wait()

    def s_send(u, p):
        send_planes(lambda to: s_snd.at[u, p, to], lambda own: s_rcv.at[u, p, own], s_ssem.at[u, p], s_rsem.at[u, p])
        s_rcv[u, p, plane] = s_snd[u, p, plane]

    def s_wait(u, p):
        wait(s_rcv.at[u, p, pl.ds(0, planes - 1)], s_rsem.at[u, p])

    def r_send(u, p):
        send_places(lambda to: r_snd.at[u, p, to], lambda own: r_rcv.at[u, p, own], r_ssem.at[u, p], r_rsem.at[u, p])
        r_rcv[u, p, place] = r_snd[u, p, place]

    def r_wait(u, p):
        wait(r_rcv.at[u, p, pl.ds(0, RING - 1)], r_rsem.at[u, p])

    def to_channels(u, p):
        s_wait(u, p)
        got = nn(gather[...], s_rcv[u, p].reshape(part * per_plane, n))
        r_snd[u, p] = got.astype(bf16).reshape(RING, mine, part, n)
        r_send(u, p)

    def to_rows(u, p):
        r_wait(u, p)
        got = nn(scatter[...], r_rcv[u, p].reshape(part * per_plane, n))
        s_snd[u, p] = got.astype(bf16).reshape(planes, PAIR * per_plane, n)
        s_send(u, p)

    def span(kt):
        return pl.ds(pl.multiple_of(kt * lanes, lanes), lanes)

    def put(u, p, kt, block):
        pieces = [block[:, h * lanes:(h + 1) * lanes].reshape(planes, per_plane, lanes) for h in range(PAIR)]
        s_snd[u, p, :, :, span(kt)] = jnp.concatenate(pieces, axis=1).astype(bf16)

    def take(u, p, kt):
        block = s_rcv[u, p, :, :, span(kt)].astype(f32)
        pieces = [block[:, h * per_plane:(h + 1) * per_plane, :].reshape(channels, lanes) for h in range(PAIR)]
        return jnp.concatenate(pieces, axis=1)

    def turned(ref, p, kt):
        return jnp.concatenate([ref[p * PAIR + h, span(kt), :].astype(f32).T for h in range(PAIR)], axis=1)

    def turn_back(ref, p, kt, block):
        for h in range(PAIR):
            ref[p * PAIR + h, span(kt), :] = block[:, h * lanes:(h + 1) * lanes].T.astype(bf16)

    def same_of(p, kt):
        ids = chain_v[:, span(kt)]
        return jnp.concatenate([(ids == chain_s[me * rows + p * PAIR + h]).astype(f32) for h in range(PAIR)], axis=1)

    def mask_of(p, kt):
        pad = pad_v[:, span(kt)]
        return jnp.concatenate([(pad * pad_s[me * rows + p * PAIR + h]).astype(f32) for h in range(PAIR)], axis=1)

    def project(u, p, kt, sig_ref, lin_ref, first):
        blk = p * chunks + kt
        both = nn(wt_in[first:first + 2 * channels, :], z[blk])
        sig, lin = sigmoid(both[:channels]), both[channels:]
        sig_ref[blk] = sig
        lin_ref[blk] = lin
        put(u, p, kt, sig * lin * mask_of(p, kt))

    for first in range(0, 4 * channels, channels):
        wt_in[first:first + channels, :] = w_in[:, first:first + channels].astype(f32).T.astype(bf16)
    wt_gate[...] = w_gate[...].astype(f32).T.astype(bf16)
    wt_out[...] = w_out[...].astype(f32).T.astype(bf16)
    bias_t[...] = jnp.broadcast_to(bias[...], (channels, channels)).T

    def start_block(p, kt):
        blk = p * chunks + kt
        col = bias_t[:, 0:1]
        values = turned(pair, p, kt) + same_of(p, kt) * col
        center = values - mean0(values)
        inverse = lax.rsqrt(mean0(center * center) + epsilon)
        z[blk] = (center * inverse).astype(bf16)
        rz[blk] = inverse
        project(B, p, kt, sig_b, lin_b, 2 * channels)

    @pl.loop(0, chunks)
    def _(kt):
        start_block(0, kt)

    pl.semaphore_wait(barrier, planes - 1 + RING - 1)
    s_send(B, 0)

    @pl.loop(1, chunks)
    def _(p):
        @pl.loop(0, chunks)
        def _(kt):
            start_block(p, kt)

        s_send(B, p)

    size = part * per_plane
    i0 = lax.broadcasted_iota(jnp.int32, (size, size), 0)
    i1 = lax.broadcasted_iota(jnp.int32, (size, size), 1)

    def at_owner(i):
        return lax.rem(i, part) * per_plane + lax.div(i, part)

    gather[...] = (i1 == at_owner(i0)).astype(f32).astype(bf16)
    scatter[...] = (i0 == at_owner(i1)).astype(f32).astype(bf16)
    j0 = lax.broadcasted_iota(jnp.int32, (n, n), 0)
    j1 = lax.broadcasted_iota(jnp.int32, (n, n), 1)

    def natural(i):
        row, own = lax.rem(i, PAIR), lax.rem(lax.div(i, PAIR), planes)
        at, p = lax.rem(lax.div(i, part), RING), lax.div(i, part * RING)
        return (own * RING + at) * rows + p * PAIR + row

    order[...] = (j0 == natural(j1)).astype(f32).astype(bf16)
    order_t[...] = (j1 == natural(j0)).astype(f32).astype(bf16)

    @pl.loop(0, chunks)
    def _(p):
        @pl.loop(0, chunks)
        def _(kt):
            project(A, p, kt, sig_a, lin_a, 0)

        s_send(A, p)
        to_channels(B, p)

    @pl.loop(0, chunks)
    def _(p):
        @pl.loop(0, chunks)
        def _(kt):
            blk = p * chunks + kt
            g = sigmoid(nn(wt_gate[...], z[blk]))
            cot = turned(gout, p, kt)
            gate[blk] = g
            gout_t[blk] = cot
            grad_u = (cot * g).astype(bf16)
            du[blk] = grad_u
            dxn[blk] = nn(w_out[...], grad_u)

        to_channels(A, p)

    @pl.loop(0, chunks)
    def _(p):
        r_wait(B, p)

    @pl.loop(0, mine)
    def _(c):
        rows_b = jnp.concatenate([r_rcv[B, p, :, c].reshape(RING * part, n) for p in range(chunks)], axis=0)
        bn[c] = nn(order[...], rows_b).astype(bf16)

    @pl.loop(0, chunks)
    def _(p):
        r_wait(A, p)

        @pl.loop(0, mine)
        def _(c):
            got = nt(r_rcv[A, p, :, c].reshape(RING * part, n), bn[c])
            r_snd[X, p, :, c] = got.astype(bf16).reshape(RING, part, n)

        r_send(X, p)

    @pl.loop(0, chunks)
    def _(p):
        to_rows(X, p)

    @pl.loop(0, chunks)
    def _(p):
        s_wait(X, p)

        @pl.loop(0, chunks)
        def _(kt):
            blk = p * chunks + kt
            values = take(X, p, kt)
            center = values - mean0(values)
            inverse = lax.rsqrt(mean0(center * center) + epsilon)
            normed = center * inverse
            xn[blk] = normed.astype(bf16)
            grad = dxn[blk]
            grad = inverse * (grad - mean0(grad) - normed * mean0(grad * normed))
            put(DX, p, kt, grad)

        s_send(DX, p)

    g_sum[...] = jnp.zeros_like(g_sum)
    chain_sum[...] = jnp.zeros_like(chain_sum)

    def add_sum(first, value):
        width = value.shape[1]
        g_sum[:, :, first:first + width] += value.reshape(planes, per_plane, width)

    @pl.loop(0, chunks)
    def _(p):
        @pl.loop(0, chunks)
        def _(kt):
            blk = p * chunks + kt
            lin = nn(wt_out[...], xn[blk])
            g = gate[blk]
            turn_back(update, p, kt, g * lin)
            grad_s = (gout_t[blk] * lin * g * (1.0 - g)).astype(bf16)
            ds[blk] = grad_s
            add_sum(4 * channels, nt(z[blk], grad_s))
            add_sum(5 * channels, nt(xn[blk], du[blk]))

        to_channels(DX, p)

    @pl.loop(0, chunks)
    def _(p):
        r_wait(DX, p)

        @pl.loop(0, mine)
        def _(c):
            grad = r_rcv[DX, p, :, c].reshape(RING * part, n)
            r_snd[DA, p, :, c] = nn(grad, bn[c]).astype(bf16).reshape(RING, part, n)
            dxt[c, p] = nt(order_t[...], grad).astype(bf16)

        r_send(DA, p)

    @pl.loop(0, mine)
    def _(c):
        total = nn(dxt[c, 0], r_rcv[A, 0, :, c].reshape(RING * part, n))
        for p in range(1, chunks):
            total = total + nn(dxt[c, p], r_rcv[A, p, :, c].reshape(RING * part, n))
        for p in range(chunks):
            r_snd[DB, p, :, c] = total[p * RING * part:(p + 1) * RING * part].astype(bf16).reshape(RING, part, n)

    @pl.loop(0, chunks)
    def _(p):
        r_send(DB, p)

    @pl.loop(0, chunks)
    def _(p):
        to_rows(DA, p)

    @pl.loop(0, chunks)
    def _(p):
        to_rows(DB, p)

    @pl.loop(0, chunks)
    def _(p):
        s_wait(DA, p)
        s_wait(DB, p)

        @pl.loop(0, chunks)
        def _(kt):
            blk = p * chunks + kt
            mask = mask_of(p, kt)
            parts = []
            for u, sig_ref, lin_ref in ((DA, sig_a, lin_a), (DB, sig_b, lin_b)):
                sig = sig_ref[blk]
                grad = take(u, p, kt) * mask * sig
                parts.append((grad * lin_ref[blk] * (1.0 - sig)).astype(bf16))
                parts.append(grad.astype(bf16))
            grad_proj = jnp.concatenate(parts, axis=0)
            normed = z[blk]
            add_sum(0, nt(normed, grad_proj))
            grad = nn(w_in[...], grad_proj) + nn(w_gate[...], ds[blk])
            normed = normed.astype(f32)
            grad = rz[blk] * (grad - mean0(grad) - normed * mean0(grad * normed))
            turn_back(gpair, p, kt, grad)
            chain_sum[...] += grad * same_of(p, kt)

    total = jnp.sum(chain_sum[...], axis=1, keepdims=True)
    add_sum(6 * channels, jnp.broadcast_to(total, (channels, channels)))

    send_planes(lambda to: g_sum.at[to], lambda own: g_rcv.at[own], g_ssem.at[0], g_rsem.at[0])
    g_rcv[plane] = g_sum[plane]
    wait(g_rcv.at[pl.ds(0, planes - 1)], g_rsem.at[0])
    h_snd[...] = jnp.sum(g_rcv[...], axis=0)
    send_places(lambda to: h_snd, lambda own: h_rcv.at[own], g_ssem.at[1], g_rsem.at[1])
    h_rcv[place] = h_snd[...]
    wait(h_rcv.at[pl.ds(0, RING - 1)], g_rsem.at[1])
    o_snd[...] = jnp.sum(h_rcv[...], axis=0) * (1.0 / n)
    send_planes(lambda to: o_snd, lambda own: o_rcv.at[own], g_ssem.at[2], g_rsem.at[2])
    o_rcv[plane] = o_snd[...]
    wait(o_rcv.at[pl.ds(0, planes - 1)], g_rsem.at[2])
    gw_in[...] = o_rcv[:, :, 0:4 * channels].reshape(channels, 4 * channels)
    gw_gate[...] = o_rcv[:, :, 4 * channels:5 * channels].reshape(channels, channels)
    gw_out[...] = o_rcv[:, :, 5 * channels:6 * channels].reshape(channels, channels)
    gw_chain[...] = o_rcv[:, :, 6 * channels:7 * channels].reshape(channels, channels).T[0:1, :]

    @pl.loop(0, 6)
    def _(u):
        @pl.loop(0, chunks)
        def _(p):
            wait(s_snd.at[u, p, pl.ds(0, planes - 1)], s_ssem.at[u, p])
            wait(r_snd.at[u, p, pl.ds(0, RING - 1)], r_ssem.at[u, p])

    wait(g_sum.at[pl.ds(0, planes - 1)], g_ssem.at[0])
    wait(h_rcv.at[pl.ds(0, RING - 1)], g_ssem.at[1])
    wait(o_rcv.at[pl.ds(0, planes - 1)], g_ssem.at[2])


def on_device(devices, pair, grad_out, pad_mask, chain_ids, chain_bias, w_in, w_gate, w_out):
    rows, n, channels = pair.shape
    planes = devices // RING
    chunks = rows // PAIR
    lanes = n // chunks
    per_plane = channels // planes
    mine = per_plane // RING
    part = planes * PAIR
    blocks = chunks * chunks
    wide = PAIR * lanes
    vmem, sems = pltpu.VMEM, pltpu.SemaphoreType.DMA
    scratch = [
        vmem((6, chunks, planes, PAIR * per_plane, n), bf16),
        vmem((6, chunks, planes, PAIR * per_plane, n), bf16),
        vmem((6, chunks, RING, mine, part, n), bf16),
        vmem((6, chunks, RING, mine, part, n), bf16),
        vmem((blocks, channels, wide), bf16),
        vmem((blocks, 1, wide), f32),
        vmem((blocks, channels, wide), f32),
        vmem((blocks, channels, wide), f32),
        vmem((blocks, channels, wide), f32),
        vmem((blocks, channels, wide), f32),
        vmem((blocks, channels, wide), f32),
        vmem((blocks, channels, wide), f32),
        vmem((blocks, channels, wide), bf16),
        vmem((blocks, channels, wide), f32),
        vmem((blocks, channels, wide), bf16),
        vmem((blocks, channels, wide), bf16),
        vmem((channels, channels), f32),
        vmem((4 * channels, channels), bf16),
        vmem((channels, channels), bf16),
        vmem((channels, channels), bf16),
        vmem((part * per_plane, part * per_plane), bf16),
        vmem((part * per_plane, part * per_plane), bf16),
        vmem((n, n), bf16),
        vmem((n, n), bf16),
        vmem((mine, n, n), bf16),
        vmem((mine, chunks, n, RING * part), bf16),
        vmem((planes, per_plane, 7 * channels), f32),
        vmem((planes, per_plane, 7 * channels), f32),
        vmem((per_plane, 7 * channels), f32),
        vmem((RING, per_plane, 7 * channels), f32),
        vmem((per_plane, 7 * channels), f32),
        vmem((planes, per_plane, 7 * channels), f32),
        vmem((channels, wide), f32),
        sems((6, chunks)), sems((6, chunks)), sems((6, chunks)), sems((6, chunks)), sems((3,)), sems((3,)),
    ]
    in_vmem = pl.BlockSpec(memory_space=pltpu.VMEM)
    in_smem = pl.BlockSpec(memory_space=pltpu.SMEM)
    shape = jax.ShapeDtypeStruct
    out = pl.pallas_call(
        functools.partial(kernel, planes),
        out_shape=(
            shape(pair.shape, bf16),
            shape(pair.shape, bf16),
            shape(w_in.shape, f32),
            shape(w_gate.shape, f32),
            shape(w_out.shape, f32),
            shape((1, channels), f32),
        ),
        in_specs=[in_vmem] * 4 + [in_smem] * 2 + [in_vmem] * 4,
        out_specs=[in_vmem] * 6,
        scratch_shapes=scratch,
        compiler_params=pltpu.CompilerParams(collective_id=0, has_side_effects=True, vmem_limit_bytes=56 * 2**20),
        cost_estimate=pl.CostEstimate(flops=2 * 10**9, bytes_accessed=3 * 10**6, transcendentals=10**6),
    )(
        pair, grad_out, pad_mask.reshape(1, n), chain_ids.reshape(1, n), pad_mask, chain_ids,
        chain_bias.reshape(1, channels), w_in, w_gate, w_out,
    )
    return (*out[:5], out[5].reshape(channels))


def solution(mesh):
    placed = (P(("dp", "dap"), None, None), P(("dp", "dap"), None, None), P("dp"), P("dp"), P(), P(), P(), P())
    return jax.shard_map(
        functools.partial(on_device, mesh.shape["dap"]),
        mesh=mesh,
        in_specs=placed,
        out_specs=(
            P(("dp", "dap"), None, None),
            P(("dp", "dap"), None, None),
            P("dp", None),
            P("dp", None),
            P("dp", None),
            P("dp"),
        ),
        check_vma=False,
    )
```

time: 1070 us -> 102 us (0.10)
  waiting for transfers between devices: 707 us -> 0 us
  blocking collectives: 138 us -> 0 us
  local copies, waits for them, and re-layouts: 111 us -> 7.79 us
  Pallas kernels: 0 us -> 93 us
  matrix products: 58 us -> 0 us
  other arithmetic: 25.5 us -> 0 us
  between operations: 14 us -> 0.66 us
    psum x1 -> x0, waiting for transfers between devices: 381 us -> none  [on_device(): lax.psum((local_w_in, local_w_gate, local_w_out, local_chain), 'dap')]
    all_gather x2 -> x0, waiting for transfers between devices: 326 us -> none  [the longest x1 210 us: on_device(): right_all = lax.all_gather(right_b, 'dap', axis=0, tiled=True)]
    psum x1 -> x0, blocking collectives: 138 us -> none  [on_device(): lax.psum((local_w_in, local_w_gate, local_w_out, local_chain), 'dap')]
    all_gather x2 -> x0, local copies, waits for them, and re-layouts: 95.3 us -> none  [the longest x1 47.9 us: on_device(): right_all = lax.all_gather(right_b, 'dap', axis=0, tiled=True)]
    pallas_call x0 -> x1, Pallas kernels: none -> 93 us  [on_device(): pl.pallas_call(functools.partial(kernel, planes), out_shape=(shape(pair.s...]
    dot_general x12 -> x0, matrix products: 58 us -> none  [the longest x1 18.6 us: on_device(): jnp.einsum('ikc,jkc->ijc', left_a, right_all, preferred_element_type=jnp....]
  transfers between devices with their start and end apart: 4 -> 0, of which waited for: 3 -> 0; matrix products, arithmetic and copies ran while one was open for 14% -> 0% of each run, Pallas kernels for 0% -> 0%
where the time goes in v1:
time: 102 us; the launch traced here: 101 us
  Pallas kernels  93 us (91%)
  local copies, waits for them, and re-layouts  7.79 us (8%)
    pallas_call x1, Pallas kernels, on_device(): pl.pallas_call(functools.partial(kernel, planes), out_shape=(shape(pair.s...  93 us
    unnamed x18, local copies, waits for them, and re-layouts  5.98 us

profile of v1, /device:TPU:1, one launch (start us, length us, event | category | flops | bytes accessed | tf_op | source)
XLA Modules:
  0.0 101.5 jit_solution(14221184901256452018)
XLA Ops:
  0.6 0.0 copy-start.4
  0.6 1.3 %reshape.24.pad_v = s32[1,384]{1,0:T(1,128)} reshape(s32[384]{0:T(512)} %pad_s.1) | data formatting | bytes 3072 | tf_op jit(solution)/shard_map/reshape | solution.py:445
  1.9 0.0 copy-done.4
  1.9 0.6 reshape.25.chain_v
  2.5 93.0 %shard_map.127 = (bf16[6,384,128]{2,1,0:T(8,128)(2,1)}, bf16[6,384,128]{2,1,0:T(8,128)(2,1)}, f32[128,512]{1,0:T(8,128)}, f32[128,128]{1,0:T(8,128)}, f32[128,128]{1,0:T(8,128)}, /*index=5*/f32[1,128]{1,0:T(1,128)}) custom-call(bf16[6,384,128]{2,1,0:T(8,128)(2,1)} %pair.1, bf16[6,384,128]{2,1,0:T(8,128)(2,1)} %gout.1, s32[1,384]{1,0:T(1,128)} %reshape.24.pad_v, ...), custom_call_target="tpu_custom_call" | custom-call | flops 2000000000 | bytes 3000000 | tf_op jit(solution)/shard_map/pallas_call | solution.py:429
  95.5 0.0 copy-start
  95.5 2.0 %copy.20 = bf16[6,384,128]{2,1,0:T(8,128)(2,1)} copy(bf16[6,384,128]{2,1,0:T(8,128)(2,1)} %get-tuple-element.24) | data formatting | bytes 1179648
  97.5 0.0 copy-done
  97.5 0.0 copy-start.1
  97.5 0.8 copy.21
  98.3 0.3 copy-done.1
  98.5 0.0 copy-start.3
  98.6 0.7 copy.22
  99.3 0.2 copy-done.3
  99.4 0.0 copy-start.2
  99.4 0.6 copy.23
  100.0 0.2 copy-done.2
  100.3 0.0 copy-start.5
  100.3 0.6 copy.24
  100.9 0.0 copy-done.5
  100.9 0.5 copy.25
Async XLA Ops:
  0.6 1.3 %copy-start.4 = (s32[384]{0:T(512)S(1)}, s32[384]{0:T(512)}, u32[]{:S(2)}) copy-start(s32[384]{0:T(512)} %chain_s.1) | copy-start | bytes 4612
  95.5 2.0 %copy-start = (bf16[6,384,128]{2,1,0:T(8,128)(2,1)S(1)}, bf16[6,384,128]{2,1,0:T(8,128)(2,1)}, u32[]{:S(2)}) copy-start(bf16[6,384,128]{2,1,0:T(8,128)(2,1)} %get-tuple-element.25) | copy-start | bytes 1769476
  97.5 1.1 %copy-start.1 = (f32[128,512]{1,0:T(8,128)S(1)}, f32[128,512]{1,0:T(8,128)}, u32[]{:S(2)}) copy-start(f32[128,512]{1,0:T(8,128)} %get-tuple-element.26) | copy-start | bytes 786436
  98.5 0.9 copy-start.3
  99.4 0.9 copy-start.2
  100.3 0.7 copy-start.5

commit v2 on v1

v2 whole, which is shorter than its diff:
```python
import functools

import jax
import jax.numpy as jnp
from jax import lax
from jax.experimental import pallas as pl
from jax.experimental.pallas import tpu as pltpu
from jax.sharding import PartitionSpec as P

epsilon = 1e-05
f32 = jnp.float32
bf16 = jnp.bfloat16

CORES = 2
QUAD = 4
PAIR = 2
B, A, X, DX, DA, DB = range(6)


def nn(left, right):
    return jnp.dot(left, right, preferred_element_type=f32)


def nt(left, right):
    return lax.dot_general(left, right, (((1,), (1,)), ((), ())), preferred_element_type=f32)


def tn(left, right):
    return lax.dot_general(left, right, (((0,), (0,)), ((), ())), preferred_element_type=f32)


def sigmoid(values):
    return 0.5 * jnp.tanh(0.5 * values) + 0.5


def mean0(values):
    return jnp.mean(values, axis=0, keepdims=True)


def kernel(
    devices,
    pair, gout, pad_v, chain_v, pad_s, chain_s, bias, w_in, w_gate, w_out,
    update_t, gpair_t, sums,
    s_snd, s_rcv, b_all, ch_a, ch_dx, ch_dxo, db_part, db_snd, db_rcv, ch_db,
    z, rz, sig_a, lin_a, sig_b, lin_b, gate, gout_t, du, acc, xn, ds,
    bias_t, wt_in, wt_gate, wt_out, gather, scatter, order, bn,
    g_sum, g_rcv, h_snd, h_rcv, o_snd, chain_sum,
    s_ssem, s_rsem, b_ssem, b_rsem, d_ssem, d_rsem, g_ssem, g_rsem,
):
    rows, n, channels = pair.shape
    planes = devices // CORES
    quads = devices // QUAD
    chunks = rows // PAIR
    lanes = n // chunks
    mine = channels // planes
    part = planes * PAIR
    size = part * mine
    me = lax.axis_index("dap")
    plane = lax.div(me, CORES)
    core = lax.rem(me, CORES)
    other = plane * CORES + 1 - core
    quad = lax.div(me, QUAD)
    corner = lax.rem(me, QUAD)

    def plane_peer(k):
        to = lax.rem(plane + k, planes)
        return to, to * CORES + core

    def quad_peer(k):
        to = lax.rem(quad + k, quads)
        return to, to * QUAD + corner

    def corner_peer(k):
        to = lax.rem(corner + k, QUAD)
        return to, quad * QUAD + to

    barrier = pltpu.get_barrier_semaphore()
    pair_core = lax.rem(corner + 1, 2)
    greeted = [plane_peer(k)[1] for k in range(1, planes)] + [quad * QUAD + pair_core, quad * QUAD + pair_core + 2]
    for device in greeted:
        pl.semaphore_signal(barrier, inc=1, device_id={"dap": device}, device_id_type=pl.DeviceIdType.MESH)

    def remote(src, dst, ssem, rsem, device):
        pltpu.make_async_remote_copy(
            src_ref=src, dst_ref=dst, send_sem=ssem, recv_sem=rsem,
            device_id={"dap": device}, device_id_type=pl.DeviceIdType.MESH,
        ).start()

    def wait(ref, sem):
        pltpu.make_async_copy(ref, ref, sem).wait()

    def s_send(u, p):
        for k in range(1, planes):
            to, device = plane_peer(k)
            remote(s_snd.at[u, p, to], s_rcv.at[u, p, plane], s_ssem.at[u, p], s_rsem.at[u, p], device)
        s_rcv[u, p, plane] = s_snd[u, p, plane]

    def s_wait(u, p):
        wait(s_rcv.at[u, p, pl.ds(0, planes - 1)], s_rsem.at[u, p])

    def to_channels(u, p):
        s_wait(u, p)
        return nn(gather[...], s_rcv[u, p].reshape(size, n)).astype(bf16)

    def to_rows(u, p, values):
        s_snd[u, p] = nn(scatter[...], values).astype(bf16).reshape(planes, PAIR * mine, n)
        s_send(u, p)

    def span(kt):
        return pl.ds(pl.multiple_of(kt * lanes, lanes), lanes)

    groups = channels // 8
    low = lax.broadcasted_iota(jnp.int32, (groups, 8, lanes), 1) < 4

    def swap(first, second):
        return (
            jnp.where(low, first, pltpu.roll(second, 4, 1)),
            jnp.where(low, pltpu.roll(first, 4, 1), second),
        )

    def put(u, p, kt, block):
        first, second = [block[:, h * lanes:(h + 1) * lanes].reshape(groups, 8, lanes) for h in range(PAIR)]
        even, odd = swap(first, second)
        s_snd[u, p, :, :, span(kt)] = jnp.stack([even, odd], axis=1).reshape(planes, 8, lanes).astype(bf16)

    def take(u, p, kt):
        block = s_rcv[u, p, :, :, span(kt)].astype(f32).reshape(groups, 2, 8, lanes)
        first, second = swap(block[:, 0], block[:, 1])
        return jnp.concatenate([first.reshape(channels, lanes), second.reshape(channels, lanes)], axis=1)

    def turned(ref, p, kt):
        return jnp.concatenate([ref[p * PAIR + h, span(kt), :].astype(f32).T for h in range(PAIR)], axis=1)

    def same_of(p, kt):
        ids = chain_v[span(kt)].reshape(1, lanes)
        return jnp.concatenate([(ids == chain_s[me * rows + p * PAIR + h]).astype(f32) for h in range(PAIR)], axis=1)

    def mask_of(p, kt):
        pad = pad_v[span(kt)].reshape(1, lanes)
        return jnp.concatenate([(pad * pad_s[me * rows + p * PAIR + h]).astype(f32) for h in range(PAIR)], axis=1)

    def project(u, p, kt, sig_ref, lin_ref, first):
        blk = p * chunks + kt
        both = nn(wt_in[first:first + 2 * channels, :], z[blk])
        sig, lin = sigmoid(both[:channels]), both[channels:]
        sig_ref[blk] = sig
        lin_ref[blk] = lin
        put(u, p, kt, sig * lin * mask_of(p, kt))

    def turn_in(first):
        wt_in[first:first + channels, :] = w_in[:, first:first + channels].astype(f32).T.astype(bf16)

    turn_in(2 * channels)
    turn_in(3 * channels)
    bias_t[...] = jnp.broadcast_to(bias[...], (channels, channels)).T

    def start_block(p, kt):
        blk = p * chunks + kt
        col = bias_t[:, 0:1]
        values = turned(pair, p, kt) + same_of(p, kt) * col
        center = values - mean0(values)
        inverse = lax.rsqrt(mean0(center * center) + epsilon)
        z[blk] = (center * inverse).astype(bf16)
        rz[blk] = inverse
        project(B, p, kt, sig_b, lin_b, 2 * channels)

    @pl.loop(0, chunks)
    def _(kt):
        start_block(0, kt)

    pl.semaphore_wait(barrier, len(greeted))
    s_send(B, 0)

    @pl.loop(1, chunks)
    def _(p):
        @pl.loop(0, chunks)
        def _(kt):
            start_block(p, kt)

        s_send(B, p)

    turn_in(0)
    turn_in(channels)

    @pl.loop(0, chunks)
    def _(p):
        @pl.loop(0, chunks)
        def _(kt):
            project(A, p, kt, sig_a, lin_a, 0)

        s_send(A, p)

    i0 = lax.broadcasted_iota(jnp.int32, (size, size), 0)
    i1 = lax.broadcasted_iota(jnp.int32, (size, size), 1)

    def at_owner(i):
        return lax.rem(i, part) * mine + lax.div(i, part)

    gather[...] = (i1 == at_owner(i0)).astype(f32).astype(bf16)
    scatter[...] = (i0 == at_owner(i1)).astype(f32).astype(bf16)
    j0 = lax.broadcasted_iota(jnp.int32, (n, n), 0)
    j1 = lax.broadcasted_iota(jnp.int32, (n, n), 1)

    def natural(i):
        row, own = lax.rem(i, PAIR), lax.rem(lax.div(i, PAIR), planes)
        p, at = lax.rem(lax.div(i, part), chunks), lax.div(i, part * chunks)
        return (own * CORES + at) * rows + p * PAIR + row

    order[...] = (j0 == natural(j1)).astype(f32).astype(bf16)
    wt_gate[...] = w_gate[...].astype(f32).T.astype(bf16)
    wt_out[...] = w_out[...].astype(f32).T.astype(bf16)

    @pl.loop(0, chunks)
    def _(p):
        b_all[core, p] = to_channels(B, p).reshape(mine, part, n)
        remote(b_all.at[core, p], b_all.at[core, p], b_ssem.at[p], b_rsem.at[p], other)

        @pl.loop(0, chunks)
        def _(kt):
            blk = p * chunks + kt
            g = sigmoid(nn(wt_gate[...], z[blk]))
            cot = turned(gout, p, kt)
            gate[blk] = g
            gout_t[blk] = cot
            grad_u = (cot * g).astype(bf16)
            du[blk] = grad_u
            acc[blk] = nn(w_out[...], grad_u)

    @pl.loop(0, chunks)
    def _(p):
        wait(b_all.at[1 - core, p], b_rsem.at[p])

    @pl.loop(0, mine)
    def _(c):
        rows_b = jnp.concatenate([b_all[at, p, c] for at in range(CORES) for p in range(chunks)], axis=0)
        bn[c] = nn(order[...], rows_b).astype(bf16)

    @pl.loop(0, chunks)
    def _(p):
        ch_a[p] = to_channels(A, p).reshape(mine, part, n)
        got = jnp.concatenate([nt(ch_a[p, c], bn[c]).astype(bf16) for c in range(mine)], axis=0)
        to_rows(X, p, got)

    g_sum[...] = jnp.zeros_like(g_sum)
    chain_sum[...] = jnp.zeros_like(chain_sum)

    def add_sum(first, value):
        width = value.shape[1]
        g_sum[:, :, first:first + width] += value.reshape(quads, channels // quads, width)

    @pl.loop(0, chunks)
    def _(p):
        s_wait(X, p)

        @pl.loop(0, chunks)
        def _(kt):
            blk = p * chunks + kt
            values = take(X, p, kt)
            center = values - mean0(values)
            inverse = lax.rsqrt(mean0(center * center) + epsilon)
            normed = center * inverse
            xn[blk] = normed.astype(bf16)
            grad = acc[blk]
            grad = inverse * (grad - mean0(grad) - normed * mean0(grad * normed))
            put(DX, p, kt, grad)

        s_send(DX, p)

        @pl.loop(0, chunks)
        def _(kt):
            blk = p * chunks + kt
            lin = nn(wt_out[...], xn[blk])
            g = gate[blk]
            update_t[blk] = (g * lin).astype(bf16)
            grad_s = (gout_t[blk] * lin * g * (1.0 - g)).astype(bf16)
            ds[blk] = grad_s
            add_sum(4 * channels, nt(z[blk], grad_s))
            add_sum(5 * channels, nt(xn[blk], du[blk]))

    @pl.loop(0, chunks)
    def _(p):
        grad = to_channels(DX, p)
        ch_dxo[p] = nn(grad, order[...]).astype(bf16).reshape(mine, part, n)
        ch_dx[p] = grad.reshape(mine, part, n)
        got = jnp.concatenate([nn(ch_dx[p, c], bn[c]).astype(bf16) for c in range(mine)], axis=0)
        to_rows(DA, p, got)

    @pl.loop(0, mine)
    def _(c):
        left = jnp.concatenate([ch_dxo[p, c] for p in range(chunks)], axis=0)
        right = jnp.concatenate([ch_a[p, c] for p in range(chunks)], axis=0)
        db_part[c] = tn(left, right).reshape(CORES, chunks * part, n)
        db_snd[c] = db_part[c, 1 - core].astype(bf16)
        remote(db_snd.at[c], db_rcv.at[c], d_ssem.at[c], d_rsem.at[c], other)

    @pl.loop(0, mine)
    def _(c):
        wait(db_rcv.at[c], d_rsem.at[c])
        total = (db_part[c, core] + db_rcv[c].astype(f32)).astype(bf16)
        for p in range(chunks):
            ch_db[p, c] = total[p * part:(p + 1) * part]

    @pl.loop(0, chunks)
    def _(p):
        to_rows(DB, p, ch_db[p].reshape(size, n))

    def grad_project(u, p, kt, sig_ref, lin_ref, first):
        blk = p * chunks + kt
        sig = sig_ref[blk]
        grad = take(u, p, kt) * mask_of(p, kt) * sig
        both = jnp.concatenate([(grad * lin_ref[blk] * (1.0 - sig)).astype(bf16), grad.astype(bf16)], axis=0)
        add_sum(first, nt(z[blk], both))
        return nn(w_in[:, first:first + 2 * channels], both)

    @pl.loop(0, chunks)
    def _(p):
        s_wait(DA, p)

        @pl.loop(0, chunks)
        def _(kt):
            blk = p * chunks + kt
            acc[blk] = grad_project(DA, p, kt, sig_a, lin_a, 0) + nn(w_gate[...], ds[blk])

    @pl.loop(0, chunks)
    def _(p):
        s_wait(DB, p)

        @pl.loop(0, chunks)
        def _(kt):
            blk = p * chunks + kt
            grad = acc[blk] + grad_project(DB, p, kt, sig_b, lin_b, 2 * channels)
            normed = z[blk].astype(f32)
            grad = rz[blk] * (grad - mean0(grad) - normed * mean0(grad * normed))
            gpair_t[blk] = grad.astype(bf16)
            chain_sum[...] += grad * same_of(p, kt)

    total = jnp.sum(chain_sum[...], axis=1, keepdims=True)
    add_sum(6 * channels, jnp.broadcast_to(total, (channels, channels)))

    def send_quads(src, dst, step):
        for k in range(1, quads):
            to, device = quad_peer(k)
            remote(src(to), dst.at[quad], g_ssem.at[step], g_rsem.at[step], device)

    send_quads(lambda to: g_sum.at[to], g_rcv, 0)
    g_rcv[quad] = g_sum[quad]
    wait(g_rcv.at[pl.ds(0, quads - 1)], g_rsem.at[0])
    h_snd[...] = jnp.sum(g_rcv[...], axis=0)
    for k in range(1, QUAD):
        remote(h_snd, h_rcv.at[corner], g_ssem.at[1], g_rsem.at[1], corner_peer(k)[1])
    h_rcv[corner] = h_snd[...]
    wait(h_rcv.at[pl.ds(0, QUAD - 1)], g_rsem.at[1])
    o_snd[...] = jnp.sum(h_rcv[...], axis=0) * (1.0 / n)
    send_quads(lambda to: o_snd, sums, 2)
    sums[quad] = o_snd[...]
    wait(sums.at[pl.ds(0, quads - 1)], g_rsem.at[2])

    @pl.loop(0, 6)
    def _(u):
        @pl.loop(0, chunks)
        def _(p):
            wait(s_snd.at[u, p, pl.ds(0, planes - 1)], s_ssem.at[u, p])

    @pl.loop(0, chunks)
    def _(p):
        wait(b_all.at[core, p], b_ssem.at[p])

    @pl.loop(0, mine)
    def _(c):
        wait(db_snd.at[c], d_ssem.at[c])

    wait(g_sum.at[pl.ds(0, quads - 1)], g_ssem.at[0])
    wait(h_rcv.at[pl.ds(0, QUAD - 1)], g_ssem.at[1])
    wait(sums.at[pl.ds(0, quads - 1)], g_ssem.at[2])


def finish(update_t, gpair_t, sums, update, gpair, gw_in, gw_gate, gw_out, gw_chain):
    rows, n, channels = update.shape
    chunks = rows // PAIR
    lanes = n // chunks
    for src, dst in ((update_t, update), (gpair_t, gpair)):
        for p in range(chunks):
            for kt in range(chunks):
                block = src[p * chunks + kt].astype(f32)
                for h in range(PAIR):
                    turned = block[:, h * lanes:(h + 1) * lanes].T
                    dst[p * PAIR + h, kt * lanes:(kt + 1) * lanes, :] = turned.astype(bf16)
    gw_in[...] = sums[:, :, 0:4 * channels].reshape(channels, 4 * channels)
    gw_gate[...] = sums[:, :, 4 * channels:5 * channels].reshape(channels, channels)
    gw_out[...] = sums[:, :, 5 * channels:6 * channels].reshape(channels, channels)
    gw_chain[...] = sums[:, :, 6 * channels:7 * channels].reshape(channels, channels).T[0:1, :]


def on_device(devices, pair, grad_out, pad_mask, chain_ids, chain_bias, w_in, w_gate, w_out):
    rows, n, channels = pair.shape
    planes, quads = devices // CORES, devices // QUAD
    chunks = rows // PAIR
    lanes = n // chunks
    mine = channels // planes
    part = planes * PAIR
    size = part * mine
    blocks = chunks * chunks
    wide = PAIR * lanes
    per_quad = channels // quads
    columns = 7 * channels
    vmem, sems = pltpu.VMEM, pltpu.SemaphoreType.DMA
    scratch = [
        vmem((6, chunks, planes, PAIR * mine, n), bf16),
        vmem((6, chunks, planes, PAIR * mine, n), bf16),
        vmem((CORES, chunks, mine, part, n), bf16),
        vmem((chunks, mine, part, n), bf16),
        vmem((chunks, mine, part, n), bf16),
        vmem((chunks, mine, part, n), bf16),
        vmem((mine, CORES, chunks * part, n), f32),
        vmem((mine, chunks * part, n), bf16),
        vmem((mine, chunks * part, n), bf16),
        vmem((chunks, mine, part, n), bf16),
        vmem((blocks, channels, wide), bf16),
        vmem((blocks, 1, wide), f32),
        vmem((blocks, channels, wide), f32),
        vmem((blocks, channels, wide), f32),
        vmem((blocks, channels, wide), f32),
        vmem((blocks, channels, wide), f32),
        vmem((blocks, channels, wide), f32),
        vmem((blocks, channels, wide), f32),
        vmem((blocks, channels, wide), bf16),
        vmem((blocks, channels, wide), f32),
        vmem((blocks, channels, wide), bf16),
        vmem((blocks, channels, wide), bf16),
        vmem((channels, channels), f32),
        vmem((4 * channels, channels), bf16),
        vmem((channels, channels), bf16),
        vmem((channels, channels), bf16),
        vmem((size, size), bf16),
        vmem((size, size), bf16),
        vmem((n, n), bf16),
        vmem((mine, n, n), bf16),
        vmem((quads, per_quad, columns), f32),
        vmem((quads, per_quad, columns), f32),
        vmem((per_quad, columns), f32),
        vmem((QUAD, per_quad, columns), f32),
        vmem((per_quad, columns), f32),
        vmem((channels, wide), f32),
        sems((6, chunks)), sems((6, chunks)), sems((chunks,)), sems((chunks,)), sems((mine,)), sems((mine,)), sems((3,)), sems((3,)),
    ]
    in_vmem = pl.BlockSpec(memory_space=pltpu.VMEM)
    in_smem = pl.BlockSpec(memory_space=pltpu.SMEM)
    shape = jax.ShapeDtypeStruct
    update_t, gpair_t, sums = pl.pallas_call(
        functools.partial(kernel, devices),
        out_shape=(
            shape((blocks, channels, wide), bf16),
            shape((blocks, channels, wide), bf16),
            shape((quads, per_quad, columns), f32),
        ),
        in_specs=[in_vmem] * 4 + [in_smem] * 2 + [in_vmem] * 4,
        out_specs=[in_vmem] * 3,
        scratch_shapes=scratch,
        compiler_params=pltpu.CompilerParams(collective_id=0, has_side_effects=True, vmem_limit_bytes=56 * 2**20),
        cost_estimate=pl.CostEstimate(flops=2 * 10**9, bytes_accessed=3 * 10**6, transcendentals=10**6),
        name="exchange",
    )(pair, grad_out, pad_mask, chain_ids, pad_mask, chain_ids, chain_bias.reshape(1, channels), w_in, w_gate, w_out)
    out = pl.pallas_call(
        finish,
        out_shape=(
            shape(pair.shape, bf16),
            shape(pair.shape, bf16),
            shape(w_in.shape, f32),
            shape(w_gate.shape, f32),
            shape(w_out.shape, f32),
            shape((1, channels), f32),
        ),
        in_specs=[in_vmem] * 3,
        out_specs=[in_vmem] * 6,
        compiler_params=pltpu.CompilerParams(vmem_limit_bytes=32 * 2**20),
        cost_estimate=pl.CostEstimate(flops=10**6, bytes_accessed=4 * 10**6, transcendentals=0),
        name="finish",
    )(update_t, gpair_t, sums)
    return (*out[:5], out[5].reshape(channels))


def solution(mesh):
    placed = (P(("dp", "dap"), None, None), P(("dp", "dap"), None, None), P("dp"), P("dp"), P(), P(), P(), P())
    return jax.shard_map(
        functools.partial(on_device, mesh.shape["dap"]),
        mesh=mesh,
        in_specs=placed,
        out_specs=(
            P(("dp", "dap"), None, None),
            P(("dp", "dap"), None, None),
            P("dp", None),
            P("dp", None),
            P("dp", None),
            P("dp"),
        ),
        check_vma=False,
    )
```

time: 102 us -> 81.7 us (0.80)
  Pallas kernels: 93 us -> 77.7 us
  local copies, waits for them, and re-layouts: 7.79 us -> 3.14 us
    pallas_call x1 -> x2, Pallas kernels: 93 us -> 77.7 us  [the longest x1 76.3 us: on_device(): pl.pallas_call(functools.partial(kernel, devices), out_shape=(shape((bloc...]
    unnamed x18 -> x6, local copies, waits for them, and re-layouts: 5.98 us -> 3.14 us
    reshape x2 -> x0, local copies, waits for them, and re-layouts: 1.81 us -> none  [the longest x1 1.25 us: on_device(): pad_mask.reshape(1, n)]
where the time goes in v2:
time: 81.7 us; the launch traced here: 81.4 us
  Pallas kernels  77.7 us (95%)
  local copies, waits for them, and re-layouts  3.14 us (4%)
    pallas_call x1, Pallas kernels, on_device(): pl.pallas_call(functools.partial(kernel, devices), out_shape=(shape((bloc...  76.3 us
    unnamed x6, local copies, waits for them, and re-layouts  3.14 us

profile of v2, /device:TPU:1, one launch (start us, length us, event | category | flops | bytes accessed | tf_op | source)
XLA Modules:
  0.0 81.4 jit_solution(4745884654860546497)
XLA Ops:
  0.6 76.3 %exchange.1 = (bf16[9,128,256]{2,1,0:T(8,128)(2,1)}, bf16[9,128,256]{2,1,0:T(8,128)(2,1)}, f32[16,8,896]{2,1,0:T(8,128)}) custom-call(bf16[6,384,128]{2,1,0:T(8,128)(2,1)} %pair.1, bf16[6,384,128]{2,1,0:T(8,128)(2,1)} %gout.1, s32[384]{0:T(512)} %pad_s.1, s32[384]{0:T(512)} %chain_s.1, s32[384]{0:T(512)} %pad_s.1, s32[384]{0:T(512)} %chain_s.1, ...), custom_call_target="tpu_custom_call" | custom-call | flops 2000000000 | bytes 3000000 | tf_op jit(solution)/shard_map/exchange/pallas_call | solution.py:449
  76.9 0.0 copy-start
  76.9 1.1 %copy-done = bf16[9,128,256]{2,1,0:T(8,128)(2,1)S(1)} copy-done((bf16[9,128,256]{2,1,0:T(8,128)(2,1)S(1)}, bf16[9,128,256]{2,1,0:T(8,128)(2,1)}, u32[]{:S(2)}) %copy-start) | copy-done | bytes 589848
  78.0 0.0 copy-start.1
  78.0 1.1 %copy-done.1 = bf16[9,128,256]{2,1,0:T(8,128)(2,1)S(1)} copy-done((bf16[9,128,256]{2,1,0:T(8,128)(2,1)S(1)}, bf16[9,128,256]{2,1,0:T(8,128)(2,1)}, u32[]{:S(2)}) %copy-start.1) | copy-done | bytes 589848
  79.0 0.0 copy-start.2
  79.0 1.0 %copy-done.2 = f32[16,8,896]{2,1,0:T(8,128)S(1)} copy-done((f32[16,8,896]{2,1,0:T(8,128)S(1)}, f32[16,8,896]{2,1,0:T(8,128)}, u32[]{:S(2)}) %copy-start.2) | copy-done | bytes 458776
  80.1 1.4 %finish.1 = (bf16[6,384,128]{2,1,0:T(8,128)(2,1)}, bf16[6,384,128]{2,1,0:T(8,128)(2,1)}, f32[128,512]{1,0:T(8,128)}, f32[128,128]{1,0:T(8,128)}, f32[128,128]{1,0:T(8,128)}, /*index=5*/f32[1,128]{1,0:T(1,128)}) custom-call(bf16[9,128,256]{2,1,0:T(8,128)(2,1)S(1)} %copy-done, bf16[9,128,256]{2,1,0:T(8,128)(2,1)S(1)} %copy-done.1, f32[16,8,896]{2,1,0:T(8,128)S(1)} %copy-done.2), custom_call_target="tpu_custom_call" | custom-call | flops 1000000 | bytes 4000000 | tf_op jit(solution)/shard_map/finish/pallas_call | solution.py:463
Async XLA Ops:
  76.9 1.1 %copy-start = (bf16[9,128,256]{2,1,0:T(8,128)(2,1)S(1)}, bf16[9,128,256]{2,1,0:T(8,128)(2,1)}, u32[]{:S(2)}) copy-start(bf16[9,128,256]{2,1,0:T(8,128)(2,1)} %get-tuple-element.15.update_t) | copy-start | bytes 1769476
  78.0 1.1 %copy-start.1 = (bf16[9,128,256]{2,1,0:T(8,128)(2,1)S(1)}, bf16[9,128,256]{2,1,0:T(8,128)(2,1)}, u32[]{:S(2)}) copy-start(bf16[9,128,256]{2,1,0:T(8,128)(2,1)} %get-tuple-element.16.gpair_t) | copy-start | bytes 1769476
  79.0 1.0 %copy-start.2 = (f32[16,8,896]{2,1,0:T(8,128)S(1)}, f32[16,8,896]{2,1,0:T(8,128)}, u32[]{:S(2)}) copy-start(f32[16,8,896]{2,1,0:T(8,128)} %get-tuple-element.17.sums) | copy-start | bytes 1376260

commit v3 on v2

--- a/solution.py
+++ b/solution.py
@@ -12,9 +12,9 @@
 bf16 = jnp.bfloat16
 
 CORES = 2
-QUAD = 4
 PAIR = 2
 B, A, X, DX, DA, DB = range(6)
+EARLY, LATE = range(2)
 
 
 def nn(left, right):
@@ -39,17 +39,17 @@
 
 def kernel(
     devices,
-    pair, gout, pad_v, chain_v, pad_s, chain_s, bias, w_in, w_gate, w_out,
-    update_t, gpair_t, sums,
-    s_snd, s_rcv, b_all, ch_a, ch_dx, ch_dxo, db_part, db_snd, db_rcv, ch_db,
+    pair_hbm, gout_hbm, pad_hbm, chain_hbm, bias_hbm, w_in_hbm, w_gate_hbm, w_out_hbm,
+    update, gpair, sums,
+    pair, gout, pad_v, chain_v, pad_s, chain_s, bias, w_in, w_gate, w_out, in_sem,
+    update_v, gpair_v, s_snd, s_rcv, b_all, ch_a, ch_dx, ch_dxo, db_part, db_snd, db_rcv, ch_db,
     z, rz, sig_a, lin_a, sig_b, lin_b, gate, gout_t, du, acc, xn, ds,
     bias_t, wt_in, wt_gate, wt_out, gather, scatter, order, bn,
-    g_sum, g_rcv, h_snd, h_rcv, o_snd, chain_sum,
-    s_ssem, s_rsem, b_ssem, b_rsem, d_ssem, d_rsem, g_ssem, g_rsem,
+    g_sum, g_rcv, rs_snd, rs_rcv, ag_snd,
+    s_ssem, s_rsem, b_ssem, b_rsem, d_ssem, d_rsem, g_ssem, g_rsem, o_sem, own_sem,
 ):
     rows, n, channels = pair.shape
     planes = devices // CORES
-    quads = devices // QUAD
     chunks = rows // PAIR
     lanes = n // chunks
     mine = channels // planes
@@ -59,26 +59,30 @@
     plane = lax.div(me, CORES)
     core = lax.rem(me, CORES)
     other = plane * CORES + 1 - core
-    quad = lax.div(me, QUAD)
-    corner = lax.rem(me, QUAD)
 
     def plane_peer(k):
         to = lax.rem(plane + k, planes)
         return to, to * CORES + core
 
-    def quad_peer(k):
-        to = lax.rem(quad + k, quads)
-        return to, to * QUAD + corner
-
-    def corner_peer(k):
-        to = lax.rem(corner + k, QUAD)
-        return to, quad * QUAD + to
-
     barrier = pltpu.get_barrier_semaphore()
-    pair_core = lax.rem(corner + 1, 2)
-    greeted = [plane_peer(k)[1] for k in range(1, planes)] + [quad * QUAD + pair_core, quad * QUAD + pair_core + 2]
+    greeted = [lax.rem(me + k, devices) for k in range(1, devices)]
     for device in greeted:
         pl.semaphore_signal(barrier, inc=1, device_id={"dap": device}, device_id_type=pl.DeviceIdType.MESH)
+
+    loads = [
+        pltpu.make_async_copy(src, dst, in_sem.at[i])
+        for i, (src, dst) in enumerate((
+            (pad_hbm, pad_v), (chain_hbm, chain_v), (pad_hbm, pad_s), (chain_hbm, chain_s), (bias_hbm, bias), (w_in_hbm, w_in),
+            *((pair_hbm.at[pl.ds(p * PAIR, PAIR)], pair.at[pl.ds(p * PAIR, PAIR)]) for p in range(chunks)),
+            (w_gate_hbm, w_gate), (w_out_hbm, w_out), (gout_hbm, gout),
+        ))
+    ]
+    for load in loads:
+        load.start()
+
+    def loaded(count):
+        for _ in range(count):
+            loads.pop(0).wait()
 
     def remote(src, dst, ssem, rsem, device):
         pltpu.make_async_remote_copy(
@@ -89,10 +93,15 @@
     def wait(ref, sem):
         pltpu.make_async_copy(ref, ref, sem).wait()
 
+    def s_sent(step):
+        wait(s_snd.at[0, 0, pl.ds(0, planes - 1)], s_ssem.at[step])
+
     def s_send(u, p):
+        if u != B or p >= 2:
+            s_sent(u * chunks + p - 2)
         for k in range(1, planes):
             to, device = plane_peer(k)
-            remote(s_snd.at[u, p, to], s_rcv.at[u, p, plane], s_ssem.at[u, p], s_rsem.at[u, p], device)
+            remote(s_snd.at[u, p, to], s_rcv.at[u, p, plane], s_ssem.at[u * chunks + p], s_rsem.at[u, p], device)
         s_rcv[u, p, plane] = s_snd[u, p, plane]
 
     def s_wait(u, p):
@@ -130,6 +139,10 @@
 
     def turned(ref, p, kt):
         return jnp.concatenate([ref[p * PAIR + h, span(kt), :].astype(f32).T for h in range(PAIR)], axis=1)
+
+    def turn_back(ref, p, kt, block):
+        for h in range(PAIR):
+            ref[p * PAIR + h, span(kt), :] = block[:, h * lanes:(h + 1) * lanes].T.astype(bf16)
 
     def same_of(p, kt):
         ids = chain_v[span(kt)].reshape(1, lanes)
@@ -150,6 +163,7 @@
     def turn_in(first):
         wt_in[first:first + channels, :] = w_in[:, first:first + channels].astype(f32).T.astype(bf16)
 
+    loaded(6)
     turn_in(2 * channels)
     turn_in(3 * channels)
     bias_t[...] = jnp.broadcast_to(bias[...], (channels, channels)).T
@@ -164,57 +178,40 @@
         rz[blk] = inverse
         project(B, p, kt, sig_b, lin_b, 2 * channels)
 
-    @pl.loop(0, chunks)
-    def _(kt):
-        start_block(0, kt)
-
-    pl.semaphore_wait(barrier, len(greeted))
-    s_send(B, 0)
-
-    @pl.loop(1, chunks)
-    def _(p):
+    def start_chunk(p):
+        loaded(1)
+
         @pl.loop(0, chunks)
         def _(kt):
             start_block(p, kt)
 
-        s_send(B, p)
-
-    turn_in(0)
-    turn_in(channels)
-
-    @pl.loop(0, chunks)
-    def _(p):
+    def a_chunk(p):
         @pl.loop(0, chunks)
         def _(kt):
             project(A, p, kt, sig_a, lin_a, 0)
-
-        s_send(A, p)
-
-    i0 = lax.broadcasted_iota(jnp.int32, (size, size), 0)
-    i1 = lax.broadcasted_iota(jnp.int32, (size, size), 1)
 
     def at_owner(i):
         return lax.rem(i, part) * mine + lax.div(i, part)
-
-    gather[...] = (i1 == at_owner(i0)).astype(f32).astype(bf16)
-    scatter[...] = (i0 == at_owner(i1)).astype(f32).astype(bf16)
-    j0 = lax.broadcasted_iota(jnp.int32, (n, n), 0)
-    j1 = lax.broadcasted_iota(jnp.int32, (n, n), 1)
 
     def natural(i):
         row, own = lax.rem(i, PAIR), lax.rem(lax.div(i, PAIR), planes)
         p, at = lax.rem(lax.div(i, part), chunks), lax.div(i, part * chunks)
         return (own * CORES + at) * rows + p * PAIR + row
 
-    order[...] = (j0 == natural(j1)).astype(f32).astype(bf16)
-    wt_gate[...] = w_gate[...].astype(f32).T.astype(bf16)
-    wt_out[...] = w_out[...].astype(f32).T.astype(bf16)
-
-    @pl.loop(0, chunks)
-    def _(p):
+    def ones_at(down, along):
+        return (down == along).astype(f32).astype(bf16)
+
+    def down(k):
+        return lax.broadcasted_iota(jnp.int32, (k, k), 0)
+
+    def along(k):
+        return lax.broadcasted_iota(jnp.int32, (1, k), 1)
+
+    def pass_on(p):
         b_all[core, p] = to_channels(B, p).reshape(mine, part, n)
         remote(b_all.at[core, p], b_all.at[core, p], b_ssem.at[p], b_rsem.at[p], other)
 
+    def gates(p):
         @pl.loop(0, chunks)
         def _(kt):
             blk = p * chunks + kt
@@ -226,6 +223,32 @@
             du[blk] = grad_u
             acc[blk] = nn(w_out[...], grad_u)
 
+    start_chunk(0)
+    pl.semaphore_wait(barrier, len(greeted))
+    s_send(B, 0)
+    start_chunk(1)
+    s_send(B, 1)
+    start_chunk(2)
+    turn_in(0)
+    turn_in(channels)
+    a_chunk(0)
+    s_send(B, 2)
+    a_chunk(1)
+    scatter[...] = ones_at(down(size), at_owner(along(size)))
+    gather[...] = ones_at(lax.rem(down(size), part) * mine + lax.div(down(size), part), along(size))
+    s_send(A, 0)
+    pass_on(0)
+    a_chunk(2)
+    order[...] = ones_at(down(n), natural(along(n)))
+    s_send(A, 1)
+    pass_on(1)
+    loaded(3)
+    wt_gate[...] = w_gate[...].astype(f32).T.astype(bf16)
+    wt_out[...] = w_out[...].astype(f32).T.astype(bf16)
+    gates(0)
+    s_send(A, 2)
+    pass_on(2)
+
     @pl.loop(0, chunks)
     def _(p):
         wait(b_all.at[1 - core, p], b_rsem.at[p])
@@ -241,12 +264,14 @@
         got = jnp.concatenate([nt(ch_a[p, c], bn[c]).astype(bf16) for c in range(mine)], axis=0)
         to_rows(X, p, got)
 
+    @pl.loop(1, chunks)
+    def _(p):
+        gates(p)
+
+    def own(p):
+        return pl.ds(p * PAIR, PAIR)
+
     g_sum[...] = jnp.zeros_like(g_sum)
-    chain_sum[...] = jnp.zeros_like(chain_sum)
-
-    def add_sum(first, value):
-        width = value.shape[1]
-        g_sum[:, :, first:first + width] += value.reshape(quads, channels // quads, width)
 
     @pl.loop(0, chunks)
     def _(p):
@@ -271,11 +296,13 @@
             blk = p * chunks + kt
             lin = nn(wt_out[...], xn[blk])
             g = gate[blk]
-            update_t[blk] = (g * lin).astype(bf16)
+            turn_back(update_v, p, kt, g * lin)
             grad_s = (gout_t[blk] * lin * g * (1.0 - g)).astype(bf16)
             ds[blk] = grad_s
-            add_sum(4 * channels, nt(z[blk], grad_s))
-            add_sum(5 * channels, nt(xn[blk], du[blk]))
+            g_sum[EARLY, 1, :, :channels] += nt(z[blk], grad_s)
+            g_sum[EARLY, 1, :, channels:] += nt(xn[blk], du[blk])
+
+        pltpu.make_async_copy(update_v.at[own(p)], update.at[own(p)], o_sem.at[0, p]).start()
 
     @pl.loop(0, chunks)
     def _(p):
@@ -304,13 +331,11 @@
     def _(p):
         to_rows(DB, p, ch_db[p].reshape(size, n))
 
-    def grad_project(u, p, kt, sig_ref, lin_ref, first):
+    def grad_project(u, p, kt, sig_ref, lin_ref):
         blk = p * chunks + kt
         sig = sig_ref[blk]
         grad = take(u, p, kt) * mask_of(p, kt) * sig
-        both = jnp.concatenate([(grad * lin_ref[blk] * (1.0 - sig)).astype(bf16), grad.astype(bf16)], axis=0)
-        add_sum(first, nt(z[blk], both))
-        return nn(w_in[:, first:first + 2 * channels], both)
+        return jnp.concatenate([(grad * lin_ref[blk] * (1.0 - sig)).astype(bf16), grad.astype(bf16)], axis=0)
 
     @pl.loop(0, chunks)
     def _(p):
@@ -319,47 +344,70 @@
         @pl.loop(0, chunks)
         def _(kt):
             blk = p * chunks + kt
-            acc[blk] = grad_project(DA, p, kt, sig_a, lin_a, 0) + nn(w_gate[...], ds[blk])
-
-    @pl.loop(0, chunks)
-    def _(p):
+            both = grad_project(DA, p, kt, sig_a, lin_a)
+            g_sum[EARLY, 0] += nt(z[blk], both)
+            acc[blk] = nn(w_in[:, :2 * channels], both) + nn(w_gate[...], ds[blk])
+
+    def sum_cores(group):
+        remote(g_sum.at[group, 1 - core], g_rcv.at[group], g_ssem.at[group, 0], g_rsem.at[group, 0], other)
+
+    def sum_planes(group):
+        wait(g_rcv.at[group], g_rsem.at[group, 0])
+        total = g_sum[group, core] + g_rcv[group]
+        halves = [total[:, h * channels:(h + 1) * channels].reshape(groups, 8, channels) for h in range(2)]
+        rs_snd[group] = jnp.stack(swap(*halves), axis=1).reshape(planes, 8, channels)
+        for k in range(1, planes):
+            to, device = plane_peer(k)
+            remote(rs_snd.at[group, to], rs_rcv.at[group, plane], g_ssem.at[group, 1], g_rsem.at[group, 1], device)
+        rs_rcv[group, plane] = rs_snd[group, plane]
+
+    at_own = core * planes + plane
+
+    def own_rows(group):
+        return pltpu.make_async_copy(ag_snd.at[group], sums.at[group, at_own], own_sem.at[group])
+
+    def share(group):
+        wait(rs_rcv.at[group, pl.ds(0, planes - 1)], g_rsem.at[group, 1])
+        ag_snd[group] = (jnp.sum(rs_rcv[group], axis=0) * (1.0 / n)).astype(bf16)
+        for k in range(1, devices):
+            device = lax.rem(me + k, devices)
+            remote(ag_snd.at[group], sums.at[group, at_own], g_ssem.at[group, 2], g_rsem.at[group, 2], device)
+        own_rows(group).start()
+
+    def last_part(p):
         s_wait(DB, p)
 
         @pl.loop(0, chunks)
         def _(kt):
             blk = p * chunks + kt
-            grad = acc[blk] + grad_project(DB, p, kt, sig_b, lin_b, 2 * channels)
+            both = grad_project(DB, p, kt, sig_b, lin_b)
+            added = nt(z[blk], both)
+            g_sum[LATE, 0, :, :channels] += added[:, :channels]
+            g_sum[LATE, 1, :, :channels] += added[:, channels:]
+            grad = acc[blk] + nn(w_in[:, 2 * channels:], both)
             normed = z[blk].astype(f32)
             grad = rz[blk] * (grad - mean0(grad) - normed * mean0(grad * normed))
-            gpair_t[blk] = grad.astype(bf16)
-            chain_sum[...] += grad * same_of(p, kt)
-
-    total = jnp.sum(chain_sum[...], axis=1, keepdims=True)
-    add_sum(6 * channels, jnp.broadcast_to(total, (channels, channels)))
-
-    def send_quads(src, dst, step):
-        for k in range(1, quads):
-            to, device = quad_peer(k)
-            remote(src(to), dst.at[quad], g_ssem.at[step], g_rsem.at[step], device)
-
-    send_quads(lambda to: g_sum.at[to], g_rcv, 0)
-    g_rcv[quad] = g_sum[quad]
-    wait(g_rcv.at[pl.ds(0, quads - 1)], g_rsem.at[0])
-    h_snd[...] = jnp.sum(g_rcv[...], axis=0)
-    for k in range(1, QUAD):
-        remote(h_snd, h_rcv.at[corner], g_ssem.at[1], g_rsem.at[1], corner_peer(k)[1])
-    h_rcv[corner] = h_snd[...]
-    wait(h_rcv.at[pl.ds(0, QUAD - 1)], g_rsem.at[1])
-    o_snd[...] = jnp.sum(h_rcv[...], axis=0) * (1.0 / n)
-    send_quads(lambda to: o_snd, sums, 2)
-    sums[quad] = o_snd[...]
-    wait(sums.at[pl.ds(0, quads - 1)], g_rsem.at[2])
-
-    @pl.loop(0, 6)
-    def _(u):
-        @pl.loop(0, chunks)
-        def _(p):
-            wait(s_snd.at[u, p, pl.ds(0, planes - 1)], s_ssem.at[u, p])
+            turn_back(gpair_v, p, kt, grad)
+            grad = grad * same_of(p, kt)
+            g_sum[LATE, 0, :, channels:] += grad[:, :lanes]
+            g_sum[LATE, 1, :, channels:] += grad[:, lanes:]
+
+        pltpu.make_async_copy(gpair_v.at[own(p)], gpair.at[own(p)], o_sem.at[1, p]).start()
+
+    sum_cores(EARLY)
+
+    @pl.loop(0, chunks - 1)
+    def _(p):
+        last_part(p)
+
+    s_sent(DB * chunks + chunks - 2)
+    s_sent(DB * chunks + chunks - 1)
+    sum_planes(EARLY)
+    last_part(chunks - 1)
+    sum_cores(LATE)
+    sum_planes(LATE)
+    share(EARLY)
+    share(LATE)
 
     @pl.loop(0, chunks)
     def _(p):
@@ -369,31 +417,68 @@
     def _(c):
         wait(db_snd.at[c], d_ssem.at[c])
 
-    wait(g_sum.at[pl.ds(0, quads - 1)], g_ssem.at[0])
-    wait(h_rcv.at[pl.ds(0, QUAD - 1)], g_ssem.at[1])
-    wait(sums.at[pl.ds(0, quads - 1)], g_ssem.at[2])
-
-
-def finish(update_t, gpair_t, sums, update, gpair, gw_in, gw_gate, gw_out, gw_chain):
-    rows, n, channels = update.shape
-    chunks = rows // PAIR
-    lanes = n // chunks
-    for src, dst in ((update_t, update), (gpair_t, gpair)):
-        for p in range(chunks):
-            for kt in range(chunks):
-                block = src[p * chunks + kt].astype(f32)
-                for h in range(PAIR):
-                    turned = block[:, h * lanes:(h + 1) * lanes].T
-                    dst[p * PAIR + h, kt * lanes:(kt + 1) * lanes, :] = turned.astype(bf16)
-    gw_in[...] = sums[:, :, 0:4 * channels].reshape(channels, 4 * channels)
-    gw_gate[...] = sums[:, :, 4 * channels:5 * channels].reshape(channels, channels)
-    gw_out[...] = sums[:, :, 5 * channels:6 * channels].reshape(channels, channels)
-    gw_chain[...] = sums[:, :, 6 * channels:7 * channels].reshape(channels, channels).T[0:1, :]
+    for group in (EARLY, LATE):
+        wait(g_rcv.at[group], g_ssem.at[group, 0])
+        wait(rs_snd.at[group, pl.ds(0, planes - 1)], g_ssem.at[group, 1])
+        wait(sums.at[group, pl.ds(0, devices - 1)], g_ssem.at[group, 2])
+        wait(sums.at[group, pl.ds(0, devices - 1)], g_rsem.at[group, 2])
+        own_rows(group).wait()
+
+    @pl.loop(0, chunks)
+    def _(p):
+        pltpu.make_async_copy(update_v.at[own(p)], update.at[own(p)], o_sem.at[0, p]).wait()
+        pltpu.make_async_copy(gpair_v.at[own(p)], gpair.at[own(p)], o_sem.at[1, p]).wait()
+
+
+def finish(
+    update_hbm, gpair_hbm, sums_hbm, update, gpair, gw_in, gw_gate, gw_out, gw_chain,
+    sums, update_v, gpair_v, in_v, gate_v, out_v, chain_v, sem, out_sem,
+):
+    rows, _, channels = update.shape
+    groups = channels // 8
+    loads, stores = [pltpu.make_async_copy(sums_hbm, sums, sem.at[0])], []
+
+    def store(src, dst):
+        stores.append(pltpu.make_async_copy(src, dst, out_sem.at[len(stores)]))
+        return stores[-1]
+
+    for src, mid, dst in ((update_hbm, update_v, update), (gpair_hbm, gpair_v, gpair)):
+        for p in range(rows // PAIR):
+            here = pl.ds(p * PAIR, PAIR)
+            loads.append(pltpu.make_async_copy(src.at[here], mid.at[here], sem.at[len(loads)]))
+            store(mid.at[here], dst.at[here])
+    for load in loads:
+        load.start()
+    loads[0].wait()
+    low = lax.broadcasted_iota(jnp.int32, (groups, 8, channels), 1) < 4
+
+    def whole(group, at):
+        planes = sums.shape[1] // CORES
+        block = sums[group, at * planes:(at + 1) * planes].astype(f32).reshape(groups, 2, 8, channels)
+        even, odd = block[:, 0], block[:, 1]
+        first = jnp.where(low, even, pltpu.roll(odd, 4, 1))
+        second = jnp.where(low, pltpu.roll(even, 4, 1), odd)
+        return first.reshape(channels, channels), second.reshape(channels, channels)
+
+    for load, out in zip(loads[1:], list(stores)):
+        load.wait()
+        out.start()
+    gate_a, lin_a = whole(EARLY, 0)
+    gate_v[...], out_v[...] = whole(EARLY, 1)
+    gate_b, chain_0 = whole(LATE, 0)
+    lin_b, chain_1 = whole(LATE, 1)
+    for i, part in enumerate((gate_a, lin_a, gate_b, lin_b)):
+        in_v[:, i * channels:(i + 1) * channels] = part
+    chain_v[...] = jnp.sum((chain_0 + chain_1).T, axis=0, keepdims=True)
+    for src, dst in ((in_v, gw_in), (gate_v, gw_gate), (out_v, gw_out), (chain_v, gw_chain)):
+        store(src, dst).start()
+    for out in stores:
+        out.wait()
 
 
 def on_device(devices, pair, grad_out, pad_mask, chain_ids, chain_bias, w_in, w_gate, w_out):
     rows, n, channels = pair.shape
-    planes, quads = devices // CORES, devices // QUAD
+    planes = devices // CORES
     chunks = rows // PAIR
     lanes = n // chunks
     mine = channels // planes
@@ -401,10 +486,21 @@
     size = part * mine
     blocks = chunks * chunks
     wide = PAIR * lanes
-    per_quad = channels // quads
-    columns = 7 * channels
     vmem, sems = pltpu.VMEM, pltpu.SemaphoreType.DMA
     scratch = [
+        vmem(pair.shape, bf16),
+        vmem(pair.shape, bf16),
+        vmem((n,), jnp.int32),
+        vmem((n,), jnp.int32),
+        pltpu.SMEM((n,), jnp.int32),
+        pltpu.SMEM((n,), jnp.int32),
+        vmem((1, channels), f32),
+        vmem(w_in.shape, bf16),
+        vmem(w_gate.shape, bf16),
+        vmem(w_out.shape, bf16),
+        sems((9 + chunks,)),
+        vmem(pair.shape, bf16),
+        vmem(pair.shape, bf16),
         vmem((6, chunks, planes, PAIR * mine, n), bf16),
         vmem((6, chunks, planes, PAIR * mine, n), bf16),
         vmem((CORES, chunks, mine, part, n), bf16),
@@ -435,31 +531,30 @@
         vmem((size, size), bf16),
         vmem((n, n), bf16),
         vmem((mine, n, n), bf16),
-        vmem((quads, per_quad, columns), f32),
-        vmem((quads, per_quad, columns), f32),
-        vmem((per_quad, columns), f32),
-        vmem((QUAD, per_quad, columns), f32),
-        vmem((per_quad, columns), f32),
-        vmem((channels, wide), f32),
-        sems((6, chunks)), sems((6, chunks)), sems((chunks,)), sems((chunks,)), sems((mine,)), sems((mine,)), sems((3,)), sems((3,)),
+        vmem((2, CORES, channels, 2 * channels), f32),
+        vmem((2, channels, 2 * channels), f32),
+        vmem((2, planes, 8, channels), f32),
+        vmem((2, planes, 8, channels), f32),
+        vmem((2, 8, channels), bf16),
+        sems((6 * chunks,)), sems((6, chunks)), sems((chunks,)), sems((chunks,)), sems((mine,)), sems((mine,)),
+        sems((2, 3)), sems((2, 3)), sems((2, chunks)), sems((2,)),
     ]
-    in_vmem = pl.BlockSpec(memory_space=pltpu.VMEM)
-    in_smem = pl.BlockSpec(memory_space=pltpu.SMEM)
+    in_any = pl.BlockSpec(memory_space=pl.ANY)
     shape = jax.ShapeDtypeStruct
-    update_t, gpair_t, sums = pl.pallas_call(
+    update, gpair, sums = pl.pallas_call(
         functools.partial(kernel, devices),
         out_shape=(
-            shape((blocks, channels, wide), bf16),
-            shape((blocks, channels, wide), bf16),
-            shape((quads, per_quad, columns), f32),
+            shape(pair.shape, bf16),
+            shape(pair.shape, bf16),
+            shape((2, devices, 8, channels), bf16),
         ),
-        in_specs=[in_vmem] * 4 + [in_smem] * 2 + [in_vmem] * 4,
-        out_specs=[in_vmem] * 3,
+        in_specs=[in_any] * 8,
+        out_specs=[in_any] * 3,
         scratch_shapes=scratch,
         compiler_params=pltpu.CompilerParams(collective_id=0, has_side_effects=True, vmem_limit_bytes=56 * 2**20),
         cost_estimate=pl.CostEstimate(flops=2 * 10**9, bytes_accessed=3 * 10**6, transcendentals=10**6),
         name="exchange",
-    )(pair, grad_out, pad_mask, chain_ids, pad_mask, chain_ids, chain_bias.reshape(1, channels), w_in, w_gate, w_out)
+    )(pair, grad_out, pad_mask, chain_ids, chain_bias.reshape(1, channels), w_in, w_gate, w_out)
     out = pl.pallas_call(
         finish,
         out_shape=(
@@ -470,12 +565,17 @@
             shape(w_out.shape, f32),
             shape((1, channels), f32),
         ),
-        in_specs=[in_vmem] * 3,
-        out_specs=[in_vmem] * 6,
-        compiler_params=pltpu.CompilerParams(vmem_limit_bytes=32 * 2**20),
+        in_specs=[in_any] * 3,
+        out_specs=[in_any] * 6,
+        scratch_shapes=[
+            vmem((2, devices, 8, channels), bf16), vmem(pair.shape, bf16), vmem(pair.shape, bf16),
+            vmem(w_in.shape, f32), vmem(w_gate.shape, f32), vmem(w_out.shape, f32), vmem((1, channels), f32),
+            sems((1 + 2 * chunks,)), sems((4 + 2 * chunks,)),
+        ],
+        compiler_params=pltpu.CompilerParams(vmem_limit_bytes=56 * 2**20),
         cost_estimate=pl.CostEstimate(flops=10**6, bytes_accessed=4 * 10**6, transcendentals=0),
         name="finish",
-    )(update_t, gpair_t, sums)
+    )(update, gpair, sums)
     return (*out[:5], out[5].reshape(channels))
 
 

time: 81.7 us -> 70.4 us (0.86)
  Pallas kernels: 77.7 us -> 69.6 us
  local copies, waits for them, and re-layouts: 3.14 us -> 0 us
    pallas_call x1, Pallas kernels: 76.3 us -> 67.2 us  [on_device(): pl.pallas_call(functools.partial(kernel, devices), out_shape=(shape(pair....]
    unnamed x6 -> x0, local copies, waits for them, and re-layouts: 3.14 us -> none
    pallas_call x1, Pallas kernels: 1.38 us -> 2.34 us  [on_device(): pl.pallas_call(finish, out_shape=(shape(pair.shape, bf16), shape(pair.sha...]
where the time goes in v3:
time: 70.4 us; the launch traced here: 70.2 us
  Pallas kernels  69.6 us (99%)
    pallas_call x1, Pallas kernels, on_device(): pl.pallas_call(functools.partial(kernel, devices), out_shape=(shape(pair....  67.2 us
    pallas_call x1, Pallas kernels, on_device(): pl.pallas_call(finish, out_shape=(shape(pair.shape, bf16), shape(pair.sha...  2.34 us

profile of v3, /device:TPU:1, one launch (start us, length us, event | category | flops | bytes accessed | tf_op | source)
XLA Modules:
  0.0 70.2 jit_solution(15272266315494304705)
XLA Ops:
  0.6 67.2 %exchange.1 = (bf16[6,384,128]{2,1,0:T(8,128)(2,1)}, bf16[6,384,128]{2,1,0:T(8,128)(2,1)}, bf16[2,64,8,128]{3,2,1,0:T(8,128)(2,1)}) custom-call(bf16[6,384,128]{2,1,0:T(8,128)(2,1)} %pair_hbm.1, bf16[6,384,128]{2,1,0:T(8,128)(2,1)} %gout_hbm.1, s32[384]{0:T(512)} %pad_hbm.1, s32[384]{0:T(512)} %chain_hbm.1, f32[1,128]{1,0:T(1,128)} %bitcast.2, ...), custom_call_target="tpu_custom_call" | custom-call | flops 2000000000 | bytes 3000000 | tf_op jit(solution)/shard_map/exchange/pallas_call | solution.py:544
  67.9 2.3 %finish.1 = (bf16[6,384,128]{2,1,0:T(8,128)(2,1)}, bf16[6,384,128]{2,1,0:T(8,128)(2,1)}, f32[128,512]{1,0:T(8,128)}, f32[128,128]{1,0:T(8,128)}, f32[128,128]{1,0:T(8,128)}, /*index=5*/f32[1,128]{1,0:T(1,128)}) custom-call(bf16[6,384,128]{2,1,0:T(8,128)(2,1)} %get-tuple-element.15.update_hbm, bf16[6,384,128]{2,1,0:T(8,128)(2,1)} %get-tuple-element.16.gpair_hbm, ...), custom_call_target="tpu_custom_call" | custom-call | flops 1000000 | bytes 4000000 | tf_op jit(solution)/shard_map/finish/pallas_call | solution.py:558

commit v4 on v3

--- a/solution.py
+++ b/solution.py
@@ -40,13 +40,14 @@
 def kernel(
     devices,
     pair_hbm, gout_hbm, pad_hbm, chain_hbm, bias_hbm, w_in_hbm, w_gate_hbm, w_out_hbm,
-    update, gpair, sums,
+    update, gpair, sums_early, sums_late, chain_out,
     pair, gout, pad_v, chain_v, pad_s, chain_s, bias, w_in, w_gate, w_out, in_sem,
-    update_v, gpair_v, s_snd, s_rcv, b_all, ch_a, ch_dx, ch_dxo, db_part, db_snd, db_rcv, ch_db,
+    update_v, gpair_v, s_snd, s_rcv, b_all, ch_a, ch_dx, db_part, db_snd, db_rcv, ch_db,
     z, rz, sig_a, lin_a, sig_b, lin_b, gate, gout_t, du, acc, xn, ds,
-    bias_t, wt_in, wt_gate, wt_out, gather, scatter, order, bn,
-    g_sum, g_rcv, rs_snd, rs_rcv, ag_snd,
-    s_ssem, s_rsem, b_ssem, b_rsem, d_ssem, d_rsem, g_ssem, g_rsem, o_sem, own_sem,
+    bias_t, wt_in, wt_gate, wt_out, gather, scatter, order, order_t,
+    g_early, g_late, both_v, chain_sum, chain_snd, chain_rcv, chain_own, chain_other, chain_all,
+    core_early, core_late, rs_early, rs_late, got_early, got_late, ag_early, ag_late,
+    s_ssem, s_rsem, b_ssem, b_rsem, d_ssem, d_rsem, g_ssem, g_rsem, o_sem, own_sem, c_sem,
 ):
     rows, n, channels = pair.shape
     planes = devices // CORES
@@ -60,12 +61,18 @@
     core = lax.rem(me, CORES)
     other = plane * CORES + 1 - core
 
+    side = 4 if planes == 32 else 2
+    offsets = [(dz, dy, dx) for dz in range(side) for dy in range(side) for dx in range(2)]
+    offsets.sort(key=lambda o: -(min(o[0], side - o[0]) + min(o[1], side - o[1]) + o[2]))
+    at_z, at_y, at_x = lax.div(plane, 2 * side), lax.rem(lax.div(plane, 2), side), lax.rem(plane, 2)
+
     def plane_peer(k):
-        to = lax.rem(plane + k, planes)
+        dz, dy, dx = offsets[k - 1]
+        to = (lax.rem(at_z + dz, side) * side + lax.rem(at_y + dy, side)) * 2 + lax.rem(at_x + dx, 2)
         return to, to * CORES + core
 
     barrier = pltpu.get_barrier_semaphore()
-    greeted = [lax.rem(me + k, devices) for k in range(1, devices)]
+    greeted = [plane_peer(k)[1] for k in range(1, planes)] + [other]
     for device in greeted:
         pl.semaphore_signal(barrier, inc=1, device_id={"dap": device}, device_id_type=pl.DeviceIdType.MESH)
 
@@ -202,14 +209,15 @@
         return (down == along).astype(f32).astype(bf16)
 
     def down(k):
-        return lax.broadcasted_iota(jnp.int32, (k, k), 0)
+        return lax.broadcasted_iota(jnp.int32, (k, 1), 0)
 
     def along(k):
         return lax.broadcasted_iota(jnp.int32, (1, k), 1)
 
     def pass_on(p):
-        b_all[core, p] = to_channels(B, p).reshape(mine, part, n)
-        remote(b_all.at[core, p], b_all.at[core, p], b_ssem.at[p], b_rsem.at[p], other)
+        b_all[:, core, p] = to_channels(B, p).reshape(mine, part, n)
+        here = b_all.at[:, core, p]
+        remote(here, here, b_ssem.at[p], b_rsem.at[p], other)
 
     def gates(p):
         @pl.loop(0, chunks)
@@ -236,33 +244,32 @@
     a_chunk(1)
     scatter[...] = ones_at(down(size), at_owner(along(size)))
     gather[...] = ones_at(lax.rem(down(size), part) * mine + lax.div(down(size), part), along(size))
+    pass_on(0)
     s_send(A, 0)
-    pass_on(0)
     a_chunk(2)
     order[...] = ones_at(down(n), natural(along(n)))
+    order_t[...] = ones_at(natural(down(n)), along(n))
+    pass_on(1)
     s_send(A, 1)
-    pass_on(1)
     loaded(3)
     wt_gate[...] = w_gate[...].astype(f32).T.astype(bf16)
     wt_out[...] = w_out[...].astype(f32).T.astype(bf16)
     gates(0)
+    pass_on(2)
     s_send(A, 2)
-    pass_on(2)
-
-    @pl.loop(0, chunks)
-    def _(p):
-        wait(b_all.at[1 - core, p], b_rsem.at[p])
-
-    @pl.loop(0, mine)
-    def _(c):
-        rows_b = jnp.concatenate([b_all[at, p, c] for at in range(CORES) for p in range(chunks)], axis=0)
-        bn[c] = nn(order[...], rows_b).astype(bf16)
+
+    @pl.loop(0, chunks)
+    def _(p):
+        wait(b_all.at[:, 1 - core, p], b_rsem.at[p])
+
+    def b_of(c):
+        return b_all[c].reshape(n, n)
 
     @pl.loop(0, chunks)
     def _(p):
         ch_a[p] = to_channels(A, p).reshape(mine, part, n)
-        got = jnp.concatenate([nt(ch_a[p, c], bn[c]).astype(bf16) for c in range(mine)], axis=0)
-        to_rows(X, p, got)
+        got = jnp.concatenate([nt(ch_a[p, c], b_of(c)).astype(bf16) for c in range(mine)], axis=0)
+        to_rows(X, p, nn(got, order_t[...]).astype(bf16))
 
     @pl.loop(1, chunks)
     def _(p):
@@ -271,7 +278,9 @@
     def own(p):
         return pl.ds(p * PAIR, PAIR)
 
-    g_sum[...] = jnp.zeros_like(g_sum)
+    g_early[...] = jnp.zeros_like(g_early)
+    g_late[...] = jnp.zeros_like(g_late)
+    chain_sum[...] = jnp.zeros_like(chain_sum)
 
     @pl.loop(0, chunks)
     def _(p):
@@ -299,22 +308,20 @@
             turn_back(update_v, p, kt, g * lin)
             grad_s = (gout_t[blk] * lin * g * (1.0 - g)).astype(bf16)
             ds[blk] = grad_s
-            g_sum[EARLY, 1, :, :channels] += nt(z[blk], grad_s)
-            g_sum[EARLY, 1, :, channels:] += nt(xn[blk], du[blk])
+            g_early[1, :, :channels] += nt(z[blk], grad_s)
+            g_early[1, :, channels:] += nt(xn[blk], du[blk])
 
         pltpu.make_async_copy(update_v.at[own(p)], update.at[own(p)], o_sem.at[0, p]).start()
 
     @pl.loop(0, chunks)
     def _(p):
-        grad = to_channels(DX, p)
-        ch_dxo[p] = nn(grad, order[...]).astype(bf16).reshape(mine, part, n)
-        ch_dx[p] = grad.reshape(mine, part, n)
-        got = jnp.concatenate([nn(ch_dx[p, c], bn[c]).astype(bf16) for c in range(mine)], axis=0)
+        ch_dx[p] = nn(to_channels(DX, p), order[...]).astype(bf16).reshape(mine, part, n)
+        got = jnp.concatenate([nn(ch_dx[p, c], b_of(c)).astype(bf16) for c in range(mine)], axis=0)
         to_rows(DA, p, got)
 
     @pl.loop(0, mine)
     def _(c):
-        left = jnp.concatenate([ch_dxo[p, c] for p in range(chunks)], axis=0)
+        left = jnp.concatenate([ch_dx[p, c] for p in range(chunks)], axis=0)
         right = jnp.concatenate([ch_a[p, c] for p in range(chunks)], axis=0)
         db_part[c] = tn(left, right).reshape(CORES, chunks * part, n)
         db_snd[c] = db_part[c, 1 - core].astype(bf16)
@@ -345,84 +352,111 @@
         def _(kt):
             blk = p * chunks + kt
             both = grad_project(DA, p, kt, sig_a, lin_a)
-            g_sum[EARLY, 0] += nt(z[blk], both)
+            g_early[0] += nt(z[blk], both)
             acc[blk] = nn(w_in[:, :2 * channels], both) + nn(w_gate[...], ds[blk])
 
-    def sum_cores(group):
-        remote(g_sum.at[group, 1 - core], g_rcv.at[group], g_ssem.at[group, 0], g_rsem.at[group, 0], other)
-
-    def sum_planes(group):
-        wait(g_rcv.at[group], g_rsem.at[group, 0])
-        total = g_sum[group, core] + g_rcv[group]
-        halves = [total[:, h * channels:(h + 1) * channels].reshape(groups, 8, channels) for h in range(2)]
-        rs_snd[group] = jnp.stack(swap(*halves), axis=1).reshape(planes, 8, channels)
+    grads = (g_early, g_late)
+    cores = (core_early, core_late)
+    rs_snd, rs_rcv = (rs_early, rs_late), (got_early, got_late)
+    ag_snd, sums = (ag_early, ag_late), (sums_early, sums_late)
+    others = pl.ds(0, planes - 1)
+
+    def send_rows(src, dst, group, step):
         for k in range(1, planes):
             to, device = plane_peer(k)
-            remote(rs_snd.at[group, to], rs_rcv.at[group, plane], g_ssem.at[group, 1], g_rsem.at[group, 1], device)
-        rs_rcv[group, plane] = rs_snd[group, plane]
-
-    at_own = core * planes + plane
-
-    def own_rows(group):
-        return pltpu.make_async_copy(ag_snd.at[group], sums.at[group, at_own], own_sem.at[group])
+            remote(src(to), dst.at[plane], g_ssem.at[group, step], g_rsem.at[group, step], device)
+
+    def sum_planes(group):
+        tiles = []
+        for at in range(grads[group].shape[0]):
+            halves = [grads[group][at, :, h * channels:(h + 1) * channels].reshape(groups, 8, channels) for h in range(2)]
+            tiles.append(jnp.stack(swap(*halves), axis=1).reshape(planes, 8, channels))
+        rs_snd[group][...] = jnp.concatenate(tiles, axis=1).astype(bf16)
+        send_rows(lambda to: rs_snd[group].at[to], rs_rcv[group], group, 0)
+        rs_rcv[group][plane] = rs_snd[group][plane]
+
+    def sum_cores(group):
+        wait(rs_rcv[group].at[others], g_rsem.at[group, 0])
+        cores[group][0] = jnp.sum(rs_rcv[group][...].astype(f32), axis=0) * (1.0 / n)
+        remote(cores[group].at[0], cores[group].at[1], g_ssem.at[group, 1], g_rsem.at[group, 1], other)
+
+    own_rows = [pltpu.make_async_copy(ag_snd[group], sums[group].at[plane], own_sem.at[group]) for group in (EARLY, LATE)]
 
     def share(group):
-        wait(rs_rcv.at[group, pl.ds(0, planes - 1)], g_rsem.at[group, 1])
-        ag_snd[group] = (jnp.sum(rs_rcv[group], axis=0) * (1.0 / n)).astype(bf16)
-        for k in range(1, devices):
-            device = lax.rem(me + k, devices)
-            remote(ag_snd.at[group], sums.at[group, at_own], g_ssem.at[group, 2], g_rsem.at[group, 2], device)
-        own_rows(group).start()
-
-    def last_part(p):
+        wait(cores[group].at[1], g_rsem.at[group, 1])
+        ag_snd[group][...] = (cores[group][0] + cores[group][1]).astype(bf16)
+        send_rows(lambda to: ag_snd[group], sums[group], group, 2)
+        own_rows[group].start()
+
+    def last_sums(p):
         s_wait(DB, p)
 
         @pl.loop(0, chunks)
         def _(kt):
+            both = grad_project(DB, p, kt, sig_b, lin_b)
+            both_v[kt] = both
+            g_late[0] += nt(z[p * chunks + kt], both)
+
+    def last_grads(p):
+        @pl.loop(0, chunks)
+        def _(kt):
             blk = p * chunks + kt
-            both = grad_project(DB, p, kt, sig_b, lin_b)
-            added = nt(z[blk], both)
-            g_sum[LATE, 0, :, :channels] += added[:, :channels]
-            g_sum[LATE, 1, :, :channels] += added[:, channels:]
-            grad = acc[blk] + nn(w_in[:, 2 * channels:], both)
+            grad = acc[blk] + nn(w_in[:, 2 * channels:], both_v[kt])
             normed = z[blk].astype(f32)
             grad = rz[blk] * (grad - mean0(grad) - normed * mean0(grad * normed))
             turn_back(gpair_v, p, kt, grad)
             grad = grad * same_of(p, kt)
-            g_sum[LATE, 0, :, channels:] += grad[:, :lanes]
-            g_sum[LATE, 1, :, channels:] += grad[:, lanes:]
+            chain_sum[...] += grad[:, :lanes] + grad[:, lanes:]
 
         pltpu.make_async_copy(gpair_v.at[own(p)], gpair.at[own(p)], o_sem.at[1, p]).start()
 
-    sum_cores(EARLY)
-
-    @pl.loop(0, chunks - 1)
-    def _(p):
-        last_part(p)
+    @pl.loop(0, chunks - 2)
+    def _(p):
+        last_sums(p)
+        last_grads(p)
 
     s_sent(DB * chunks + chunks - 2)
     s_sent(DB * chunks + chunks - 1)
     sum_planes(EARLY)
-    last_part(chunks - 1)
+    last_sums(chunks - 2)
+    last_grads(chunks - 2)
+    last_sums(chunks - 1)
+    sum_planes(LATE)
+    last_grads(chunks - 1)
+    chain_snd[...] = jnp.sum(chain_sum[...].T, axis=0, keepdims=True)
+    for k in range(1, planes):
+        remote(chain_snd, chain_rcv.at[plane], c_sem.at[0], c_sem.at[1], plane_peer(k)[1])
+    chain_rcv[plane] = chain_snd[...]
+    sum_cores(EARLY)
+    share(EARLY)
     sum_cores(LATE)
-    sum_planes(LATE)
-    share(EARLY)
+    wait(chain_rcv.at[others], c_sem.at[1])
+    chain_own[...] = jnp.sum(chain_rcv[...], axis=0) * (1.0 / n)
+    remote(chain_own, chain_other, c_sem.at[2], c_sem.at[3], other)
     share(LATE)
-
-    @pl.loop(0, chunks)
-    def _(p):
-        wait(b_all.at[core, p], b_ssem.at[p])
+    wait(chain_other, c_sem.at[3])
+    chain_all[...] = chain_own[...] + chain_other[...]
+    chain_copy = pltpu.make_async_copy(chain_all, chain_out, c_sem.at[4])
+    chain_copy.start()
+
+    @pl.loop(0, chunks)
+    def _(p):
+        wait(b_all.at[:, core, p], b_ssem.at[p])
 
     @pl.loop(0, mine)
     def _(c):
         wait(db_snd.at[c], d_ssem.at[c])
 
     for group in (EARLY, LATE):
-        wait(g_rcv.at[group], g_ssem.at[group, 0])
-        wait(rs_snd.at[group, pl.ds(0, planes - 1)], g_ssem.at[group, 1])
-        wait(sums.at[group, pl.ds(0, devices - 1)], g_ssem.at[group, 2])
-        wait(sums.at[group, pl.ds(0, devices - 1)], g_rsem.at[group, 2])
-        own_rows(group).wait()
+        wait(rs_snd[group].at[others], g_ssem.at[group, 0])
+        wait(cores[group].at[0], g_ssem.at[group, 1])
+        wait(sums[group].at[others], g_ssem.at[group, 2])
+        wait(sums[group].at[others], g_rsem.at[group, 2])
+        own_rows[group].wait()
+
+    wait(chain_rcv.at[others], c_sem.at[0])
+    wait(chain_own, c_sem.at[2])
+    chain_copy.wait()
 
     @pl.loop(0, chunks)
     def _(p):
@@ -431,12 +465,14 @@
 
 
 def finish(
-    update_hbm, gpair_hbm, sums_hbm, update, gpair, gw_in, gw_gate, gw_out, gw_chain,
-    sums, update_v, gpair_v, in_v, gate_v, out_v, chain_v, sem, out_sem,
+    update_hbm, gpair_hbm, early_hbm, late_hbm, chain_hbm, update, gpair, gw_in, gw_gate, gw_out, gw_chain,
+    early, late, update_v, gpair_v, in_v, gate_v, out_v, chain_v, sem, out_sem,
 ):
     rows, _, channels = update.shape
     groups = channels // 8
-    loads, stores = [pltpu.make_async_copy(sums_hbm, sums, sem.at[0])], []
+    loads, stores = [], []
+    for src, dst in ((early_hbm, early), (late_hbm, late), (chain_hbm, chain_v)):
+        loads.append(pltpu.make_async_copy(src, dst, sem.at[len(loads)]))
 
     def store(src, dst):
         stores.append(pltpu.make_async_copy(src, dst, out_sem.at[len(stores)]))
@@ -449,28 +485,25 @@
             store(mid.at[here], dst.at[here])
     for load in loads:
         load.start()
-    loads[0].wait()
     low = lax.broadcasted_iota(jnp.int32, (groups, 8, channels), 1) < 4
 
-    def whole(group, at):
-        planes = sums.shape[1] // CORES
-        block = sums[group, at * planes:(at + 1) * planes].astype(f32).reshape(groups, 2, 8, channels)
+    def whole(sums, at):
+        block = sums[...].astype(f32)[:, at * 8:(at + 1) * 8].reshape(groups, 2, 8, channels)
         even, odd = block[:, 0], block[:, 1]
         first = jnp.where(low, even, pltpu.roll(odd, 4, 1))
         second = jnp.where(low, pltpu.roll(even, 4, 1), odd)
         return first.reshape(channels, channels), second.reshape(channels, channels)
 
-    for load, out in zip(loads[1:], list(stores)):
+    for load, out in zip(loads[3:], list(stores)):
         load.wait()
         out.start()
-    gate_a, lin_a = whole(EARLY, 0)
-    gate_v[...], out_v[...] = whole(EARLY, 1)
-    gate_b, chain_0 = whole(LATE, 0)
-    lin_b, chain_1 = whole(LATE, 1)
-    for i, part in enumerate((gate_a, lin_a, gate_b, lin_b)):
+    for load in loads[:3]:
+        load.wait()
+    store(chain_v, gw_chain).start()
+    gate_v[...], out_v[...] = whole(early, 1)
+    for i, part in enumerate(whole(early, 0) + whole(late, 0)):
         in_v[:, i * channels:(i + 1) * channels] = part
-    chain_v[...] = jnp.sum((chain_0 + chain_1).T, axis=0, keepdims=True)
-    for src, dst in ((in_v, gw_in), (gate_v, gw_gate), (out_v, gw_out), (chain_v, gw_chain)):
+    for src, dst in ((in_v, gw_in), (gate_v, gw_gate), (out_v, gw_out)):
         store(src, dst).start()
     for out in stores:
         out.wait()
@@ -503,8 +536,7 @@
         vmem(pair.shape, bf16),
         vmem((6, chunks, planes, PAIR * mine, n), bf16),
         vmem((6, chunks, planes, PAIR * mine, n), bf16),
-        vmem((CORES, chunks, mine, part, n), bf16),
-        vmem((chunks, mine, part, n), bf16),
+        vmem((mine, CORES, chunks, part, n), bf16),
         vmem((chunks, mine, part, n), bf16),
         vmem((chunks, mine, part, n), bf16),
         vmem((mine, CORES, chunks * part, n), f32),
@@ -530,26 +562,40 @@
         vmem((size, size), bf16),
         vmem((size, size), bf16),
         vmem((n, n), bf16),
-        vmem((mine, n, n), bf16),
-        vmem((2, CORES, channels, 2 * channels), f32),
+        vmem((n, n), bf16),
         vmem((2, channels, 2 * channels), f32),
-        vmem((2, planes, 8, channels), f32),
-        vmem((2, planes, 8, channels), f32),
-        vmem((2, 8, channels), bf16),
+        vmem((1, channels, 2 * channels), f32),
+        vmem((chunks, 2 * channels, wide), bf16),
+        vmem((channels, lanes), f32),
+        vmem((1, channels), f32),
+        vmem((planes, 1, channels), f32),
+        vmem((1, channels), f32),
+        vmem((1, channels), f32),
+        vmem((1, channels), f32),
+        vmem((2, 16, channels), f32),
+        vmem((2, 8, channels), f32),
+        vmem((planes, 16, channels), bf16),
+        vmem((planes, 8, channels), bf16),
+        vmem((planes, 16, channels), bf16),
+        vmem((planes, 8, channels), bf16),
+        vmem((16, channels), bf16),
+        vmem((8, channels), bf16),
         sems((6 * chunks,)), sems((6, chunks)), sems((chunks,)), sems((chunks,)), sems((mine,)), sems((mine,)),
-        sems((2, 3)), sems((2, 3)), sems((2, chunks)), sems((2,)),
+        sems((2, 3)), sems((2, 3)), sems((2, chunks)), sems((2,)), sems((5,)),
     ]
     in_any = pl.BlockSpec(memory_space=pl.ANY)
     shape = jax.ShapeDtypeStruct
-    update, gpair, sums = pl.pallas_call(
+    results = pl.pallas_call(
         functools.partial(kernel, devices),
         out_shape=(
             shape(pair.shape, bf16),
             shape(pair.shape, bf16),
-            shape((2, devices, 8, channels), bf16),
+            shape((planes, 16, channels), bf16),
+            shape((planes, 8, channels), bf16),
+            shape((1, channels), f32),
         ),
         in_specs=[in_any] * 8,
-        out_specs=[in_any] * 3,
+        out_specs=[in_any] * 5,
         scratch_shapes=scratch,
         compiler_params=pltpu.CompilerParams(collective_id=0, has_side_effects=True, vmem_limit_bytes=56 * 2**20),
         cost_estimate=pl.CostEstimate(flops=2 * 10**9, bytes_accessed=3 * 10**6, transcendentals=10**6),
@@ -565,17 +611,17 @@
             shape(w_out.shape, f32),
             shape((1, channels), f32),
         ),
-        in_specs=[in_any] * 3,
+        in_specs=[in_any] * 5,
         out_specs=[in_any] * 6,
         scratch_shapes=[
-            vmem((2, devices, 8, channels), bf16), vmem(pair.shape, bf16), vmem(pair.shape, bf16),
+            vmem((planes, 16, channels), bf16), vmem((planes, 8, channels), bf16), vmem(pair.shape, bf16), vmem(pair.shape, bf16),
             vmem(w_in.shape, f32), vmem(w_gate.shape, f32), vmem(w_out.shape, f32), vmem((1, channels), f32),
-            sems((1 + 2 * chunks,)), sems((4 + 2 * chunks,)),
+            sems((3 + 2 * chunks,)), sems((4 + 2 * chunks,)),
         ],
         compiler_params=pltpu.CompilerParams(vmem_limit_bytes=56 * 2**20),
         cost_estimate=pl.CostEstimate(flops=10**6, bytes_accessed=4 * 10**6, transcendentals=0),
         name="finish",
-    )(update, gpair, sums)
+    )(*results)
     return (*out[:5], out[5].reshape(channels))
 
 

time: 70.4 us -> 67.3 us (0.956)
  Pallas kernels: 69.6 us -> 66.5 us
    pallas_call x1, Pallas kernels: 67.2 us -> 64.1 us  [on_device(): pl.pallas_call(functools.partial(kernel, devices), out_shape=(shape(pair....]
where the time goes in v4:
time: 67.3 us; the launch traced here: 67.2 us
  Pallas kernels  66.5 us (99%)
    pallas_call x1, Pallas kernels, on_device(): pl.pallas_call(functools.partial(kernel, devices), out_shape=(shape(pair....  64.1 us
    pallas_call x1, Pallas kernels, on_device(): pl.pallas_call(finish, out_shape=(shape(pair.shape, bf16), shape(pair.sha...  2.39 us

profile of v4, /device:TPU:1, one launch (start us, length us, event | category | flops | bytes accessed | tf_op | source)
XLA Modules:
  0.0 67.2 jit_solution(6277100204662784310)
XLA Ops:
  0.6 64.1 %exchange.1 = (bf16[6,384,128]{2,1,0:T(8,128)(2,1)}, bf16[6,384,128]{2,1,0:T(8,128)(2,1)}, bf16[32,16,128]{2,1,0:T(8,128)(2,1)}, bf16[32,8,128]{2,1,0:T(8,128)(2,1)}, f32[1,128]{1,0:T(1,128)}) custom-call(bf16[6,384,128]{2,1,0:T(8,128)(2,1)} %pair_hbm.1, bf16[6,384,128]{2,1,0:T(8,128)(2,1)} %gout_hbm.1, s32[384]{0:T(512)} %pad_hbm.1, s32[384]{0:T(512)} %chain_hbm.1, ...), custom_call_target="tpu_custom_call" | custom-call | flops 2000000000 | bytes 3000000 | tf_op jit(solution)/shard_map/exchange/pallas_call | solution.py:588
  64.8 2.4 %finish.1 = (bf16[6,384,128]{2,1,0:T(8,128)(2,1)}, bf16[6,384,128]{2,1,0:T(8,128)(2,1)}, f32[128,512]{1,0:T(8,128)}, f32[128,128]{1,0:T(8,128)}, f32[128,128]{1,0:T(8,128)}, /*index=5*/f32[1,128]{1,0:T(1,128)}) custom-call(bf16[6,384,128]{2,1,0:T(8,128)(2,1)} %get-tuple-element.17.update_hbm, bf16[6,384,128]{2,1,0:T(8,128)(2,1)} %get-tuple-element.18.gpair_hbm, ...), custom_call_target="tpu_custom_call" | custom-call | flops 1000000 | bytes 4000000 | tf_op jit(solution)/shard_map/finish/pallas_call | solution.py:604

commit v5 on v4

--- a/solution.py
+++ b/solution.py
@@ -42,12 +42,12 @@
     pair_hbm, gout_hbm, pad_hbm, chain_hbm, bias_hbm, w_in_hbm, w_gate_hbm, w_out_hbm,
     update, gpair, sums_early, sums_late, chain_out,
     pair, gout, pad_v, chain_v, pad_s, chain_s, bias, w_in, w_gate, w_out, in_sem,
-    update_v, gpair_v, s_snd, s_rcv, b_all, ch_a, ch_dx, db_part, db_snd, db_rcv, ch_db,
+    s_snd, s_rcv, b_all, ch_a, ch_dx, db_part, db_snd, db_rcv, ch_db,
     z, rz, sig_a, lin_a, sig_b, lin_b, gate, gout_t, du, acc, xn, ds,
     bias_t, wt_in, wt_gate, wt_out, gather, scatter, order, order_t,
-    g_early, g_late, both_v, chain_sum, chain_snd, chain_rcv, chain_own, chain_other, chain_all,
+    g_early, g_late, both_v, chain_sum, chain_snd, chain_rcv, chain_own, chain_other,
     core_early, core_late, rs_early, rs_late, got_early, got_late, ag_early, ag_late,
-    s_ssem, s_rsem, b_ssem, b_rsem, d_ssem, d_rsem, g_ssem, g_rsem, o_sem, own_sem, c_sem,
+    s_ssem, s_rsem, b_ssem, b_rsem, d_ssem, d_rsem, g_ssem, g_rsem, c_sem,
 ):
     rows, n, channels = pair.shape
     planes = devices // CORES
@@ -275,9 +275,6 @@
     def _(p):
         gates(p)
 
-    def own(p):
-        return pl.ds(p * PAIR, PAIR)
-
     g_early[...] = jnp.zeros_like(g_early)
     g_late[...] = jnp.zeros_like(g_late)
     chain_sum[...] = jnp.zeros_like(chain_sum)
@@ -305,13 +302,11 @@
             blk = p * chunks + kt
             lin = nn(wt_out[...], xn[blk])
             g = gate[blk]
-            turn_back(update_v, p, kt, g * lin)
+            turn_back(update, p, kt, g * lin)
             grad_s = (gout_t[blk] * lin * g * (1.0 - g)).astype(bf16)
             ds[blk] = grad_s
             g_early[1, :, :channels] += nt(z[blk], grad_s)
             g_early[1, :, channels:] += nt(xn[blk], du[blk])
-
-        pltpu.make_async_copy(update_v.at[own(p)], update.at[own(p)], o_sem.at[0, p]).start()
 
     @pl.loop(0, chunks)
     def _(p):
@@ -380,13 +375,11 @@
         cores[group][0] = jnp.sum(rs_rcv[group][...].astype(f32), axis=0) * (1.0 / n)
         remote(cores[group].at[0], cores[group].at[1], g_ssem.at[group, 1], g_rsem.at[group, 1], other)
 
-    own_rows = [pltpu.make_async_copy(ag_snd[group], sums[group].at[plane], own_sem.at[group]) for group in (EARLY, LATE)]
-
     def share(group):
         wait(cores[group].at[1], g_rsem.at[group, 1])
         ag_snd[group][...] = (cores[group][0] + cores[group][1]).astype(bf16)
         send_rows(lambda to: ag_snd[group], sums[group], group, 2)
-        own_rows[group].start()
+        sums[group][plane] = ag_snd[group][...]
 
     def last_sums(p):
         s_wait(DB, p)
@@ -404,11 +397,9 @@
             grad = acc[blk] + nn(w_in[:, 2 * channels:], both_v[kt])
             normed = z[blk].astype(f32)
             grad = rz[blk] * (grad - mean0(grad) - normed * mean0(grad * normed))
-            turn_back(gpair_v, p, kt, grad)
+            turn_back(gpair, p, kt, grad)
             grad = grad * same_of(p, kt)
             chain_sum[...] += grad[:, :lanes] + grad[:, lanes:]
-
-        pltpu.make_async_copy(gpair_v.at[own(p)], gpair.at[own(p)], o_sem.at[1, p]).start()
 
     @pl.loop(0, chunks - 2)
     def _(p):
@@ -435,9 +426,7 @@
     remote(chain_own, chain_other, c_sem.at[2], c_sem.at[3], other)
     share(LATE)
     wait(chain_other, c_sem.at[3])
-    chain_all[...] = chain_own[...] + chain_other[...]
-    chain_copy = pltpu.make_async_copy(chain_all, chain_out, c_sem.at[4])
-    chain_copy.start()
+    chain_out[...] = chain_own[...] + chain_other[...]
 
     @pl.loop(0, chunks)
     def _(p):
@@ -452,39 +441,26 @@
         wait(cores[group].at[0], g_ssem.at[group, 1])
         wait(sums[group].at[others], g_ssem.at[group, 2])
         wait(sums[group].at[others], g_rsem.at[group, 2])
-        own_rows[group].wait()
 
     wait(chain_rcv.at[others], c_sem.at[0])
     wait(chain_own, c_sem.at[2])
-    chain_copy.wait()
-
-    @pl.loop(0, chunks)
-    def _(p):
-        pltpu.make_async_copy(update_v.at[own(p)], update.at[own(p)], o_sem.at[0, p]).wait()
-        pltpu.make_async_copy(gpair_v.at[own(p)], gpair.at[own(p)], o_sem.at[1, p]).wait()
 
 
 def finish(
-    update_hbm, gpair_hbm, early_hbm, late_hbm, chain_hbm, update, gpair, gw_in, gw_gate, gw_out, gw_chain,
-    early, late, update_v, gpair_v, in_v, gate_v, out_v, chain_v, sem, out_sem,
+    update_v, gpair_v, early, late, chain, update, gpair, gw_in, gw_gate, gw_out, gw_chain,
+    in_v, gate_v, out_v, out_sem,
 ):
-    rows, _, channels = update.shape
+    channels = update.shape[2]
     groups = channels // 8
-    loads, stores = [], []
-    for src, dst in ((early_hbm, early), (late_hbm, late), (chain_hbm, chain_v)):
-        loads.append(pltpu.make_async_copy(src, dst, sem.at[len(loads)]))
+    stores = []
 
     def store(src, dst):
         stores.append(pltpu.make_async_copy(src, dst, out_sem.at[len(stores)]))
-        return stores[-1]
-
-    for src, mid, dst in ((update_hbm, update_v, update), (gpair_hbm, gpair_v, gpair)):
-        for p in range(rows // PAIR):
-            here = pl.ds(p * PAIR, PAIR)
-            loads.append(pltpu.make_async_copy(src.at[here], mid.at[here], sem.at[len(loads)]))
-            store(mid.at[here], dst.at[here])
-    for load in loads:
-        load.start()
+        stores[-1].start()
+
+    store(update_v, update)
+    store(gpair_v, gpair)
+    store(chain, gw_chain)
     low = lax.broadcasted_iota(jnp.int32, (groups, 8, channels), 1) < 4
 
     def whole(sums, at):
@@ -494,17 +470,12 @@
         second = jnp.where(low, pltpu.roll(even, 4, 1), odd)
         return first.reshape(channels, channels), second.reshape(channels, channels)
 
-    for load, out in zip(loads[3:], list(stores)):
-        load.wait()
-        out.start()
-    for load in loads[:3]:
-        load.wait()
-    store(chain_v, gw_chain).start()
-    gate_v[...], out_v[...] = whole(early, 1)
     for i, part in enumerate(whole(early, 0) + whole(late, 0)):
         in_v[:, i * channels:(i + 1) * channels] = part
-    for src, dst in ((in_v, gw_in), (gate_v, gw_gate), (out_v, gw_out)):
-        store(src, dst).start()
+    store(in_v, gw_in)
+    gate_v[...], out_v[...] = whole(early, 1)
+    store(gate_v, gw_gate)
+    store(out_v, gw_out)
     for out in stores:
         out.wait()
 
@@ -532,8 +503,6 @@
         vmem(w_gate.shape, bf16),
         vmem(w_out.shape, bf16),
         sems((9 + chunks,)),
-        vmem(pair.shape, bf16),
-        vmem(pair.shape, bf16),
         vmem((6, chunks, planes, PAIR * mine, n), bf16),
         vmem((6, chunks, planes, PAIR * mine, n), bf16),
         vmem((mine, CORES, chunks, part, n), bf16),
@@ -571,7 +540,6 @@
         vmem((planes, 1, channels), f32),
         vmem((1, channels), f32),
         vmem((1, channels), f32),
-        vmem((1, channels), f32),
         vmem((2, 16, channels), f32),
         vmem((2, 8, channels), f32),
         vmem((planes, 16, channels), bf16),
@@ -581,21 +549,22 @@
         vmem((16, channels), bf16),
         vmem((8, channels), bf16),
         sems((6 * chunks,)), sems((6, chunks)), sems((chunks,)), sems((chunks,)), sems((mine,)), sems((mine,)),
-        sems((2, 3)), sems((2, 3)), sems((2, chunks)), sems((2,)), sems((5,)),
+        sems((2, 3)), sems((2, 3)), sems((4,)),
     ]
     in_any = pl.BlockSpec(memory_space=pl.ANY)
+    in_vmem = pl.BlockSpec(memory_space=pltpu.VMEM)
     shape = jax.ShapeDtypeStruct
     results = pl.pallas_call(
         functools.partial(kernel, devices),
         out_shape=(
-            shape(pair.shape, bf16),
-            shape(pair.shape, bf16),
-            shape((planes, 16, channels), bf16),
-            shape((planes, 8, channels), bf16),
-            shape((1, channels), f32),
+            vmem(pair.shape, bf16),
+            vmem(pair.shape, bf16),
+            vmem((planes, 16, channels), bf16),
+            vmem((planes, 8, channels), bf16),
+            vmem((1, channels), f32),
         ),
         in_specs=[in_any] * 8,
-        out_specs=[in_any] * 5,
+        out_specs=[in_vmem] * 5,
         scratch_shapes=scratch,
         compiler_params=pltpu.CompilerParams(collective_id=0, has_side_effects=True, vmem_limit_bytes=56 * 2**20),
         cost_estimate=pl.CostEstimate(flops=2 * 10**9, bytes_accessed=3 * 10**6, transcendentals=10**6),
@@ -611,14 +580,10 @@
             shape(w_out.shape, f32),
             shape((1, channels), f32),
         ),
-        in_specs=[in_any] * 5,
+        in_specs=[in_vmem] * 5,
         out_specs=[in_any] * 6,
-        scratch_shapes=[
-            vmem((planes, 16, channels), bf16), vmem((planes, 8, channels), bf16), vmem(pair.shape, bf16), vmem(pair.shape, bf16),
-            vmem(w_in.shape, f32), vmem(w_gate.shape, f32), vmem(w_out.shape, f32), vmem((1, channels), f32),
-            sems((3 + 2 * chunks,)), sems((4 + 2 * chunks,)),
-        ],
-        compiler_params=pltpu.CompilerParams(vmem_limit_bytes=56 * 2**20),
+        scratch_shapes=[vmem(w_in.shape, f32), vmem(w_gate.shape, f32), vmem(w_out.shape, f32), sems((6,))],
+        compiler_params=pltpu.CompilerParams(vmem_limit_bytes=16 * 2**20),
         cost_estimate=pl.CostEstimate(flops=10**6, bytes_accessed=4 * 10**6, transcendentals=0),
         name="finish",
     )(*results)

time: 67.3 us -> 65.9 us (0.979)
  Pallas kernels: 66.5 us -> 65.1 us
    pallas_call x1, Pallas kernels: 2.39 us -> 1.19 us  [on_device(): pl.pallas_call(finish, out_shape=(shape(pair.shape, bf16), shape(pair.sha...]
where the time goes in v5:
time: 65.9 us; the launch traced here: 65.8 us
  Pallas kernels  65.1 us (99%)
    pallas_call x1, Pallas kernels, on_device(): pl.pallas_call(functools.partial(kernel, devices), out_shape=(vmem(pair.s...  63.9 us

profile of v5, /device:TPU:1, one launch (start us, length us, event | category | flops | bytes accessed | tf_op | source)
XLA Modules:
  0.0 65.8 jit_solution(7031082673993751530)
XLA Ops:
  0.6 63.9 %exchange.1 = (bf16[6,384,128]{2,1,0:T(8,128)(2,1)S(1)}, bf16[6,384,128]{2,1,0:T(8,128)(2,1)S(1)}, bf16[32,16,128]{2,1,0:T(8,128)(2,1)S(1)}, bf16[32,8,128]{2,1,0:T(8,128)(2,1)S(1)}, f32[1,128]{1,0:T(1,128)S(1)}) custom-call(bf16[6,384,128]{2,1,0:T(8,128)(2,1)} %pair_hbm.1, bf16[6,384,128]{2,1,0:T(8,128)(2,1)} %gout_hbm.1, s32[384]{0:T(512)} %pad_hbm.1, ...), custom_call_target="tpu_custom_call" | custom-call | flops 2000000000 | bytes 3000000 | tf_op jit(solution)/shard_map/exchange/pallas_call | solution.py:557
  64.6 1.2 %finish.1 = (bf16[6,384,128]{2,1,0:T(8,128)(2,1)}, bf16[6,384,128]{2,1,0:T(8,128)(2,1)}, f32[128,512]{1,0:T(8,128)}, f32[128,128]{1,0:T(8,128)}, f32[128,128]{1,0:T(8,128)}, /*index=5*/f32[1,128]{1,0:T(1,128)}) custom-call(bf16[6,384,128]{2,1,0:T(8,128)(2,1)S(1)} %get-tuple-element.17.update_v, bf16[6,384,128]{2,1,0:T(8,128)(2,1)S(1)} %get-tuple-element.18.gpair_v, ...), custom_call_target="tpu_custom_call" | custom-call | flops 1000000 | bytes 4000000 | tf_op jit(solution)/shard_map/finish/pallas_call | solution.py:573

commit v6 on v5

--- a/solution.py
+++ b/solution.py
@@ -46,7 +46,7 @@
     z, rz, sig_a, lin_a, sig_b, lin_b, gate, gout_t, du, acc, xn, ds,
     bias_t, wt_in, wt_gate, wt_out, gather, scatter, order, order_t,
     g_early, g_late, both_v, chain_sum, chain_snd, chain_rcv, chain_own, chain_other,
-    core_early, core_late, rs_early, rs_late, got_early, got_late, ag_early, ag_late,
+    core_early, rs_early, rs_late, got_early, got_late, ag_early, ag_late,
     s_ssem, s_rsem, b_ssem, b_rsem, d_ssem, d_rsem, g_ssem, g_rsem, c_sem,
 ):
     rows, n, channels = pair.shape
@@ -72,7 +72,7 @@
         return to, to * CORES + core
 
     barrier = pltpu.get_barrier_semaphore()
-    greeted = [plane_peer(k)[1] for k in range(1, planes)] + [other]
+    greeted = [plane_peer(k)[1] for k in range(1, planes)] + [plane_peer(k)[1] + 1 - 2 * core for k in range(1, planes)] + [other]
     for device in greeted:
         pl.semaphore_signal(barrier, inc=1, device_id={"dap": device}, device_id_type=pl.DeviceIdType.MESH)
 
@@ -104,8 +104,6 @@
         wait(s_snd.at[0, 0, pl.ds(0, planes - 1)], s_ssem.at[step])
 
     def s_send(u, p):
-        if u != B or p >= 2:
-            s_sent(u * chunks + p - 2)
         for k in range(1, planes):
             to, device = plane_peer(k)
             remote(s_snd.at[u, p, to], s_rcv.at[u, p, plane], s_ssem.at[u * chunks + p], s_rsem.at[u, p], device)
@@ -351,7 +349,6 @@
             acc[blk] = nn(w_in[:, :2 * channels], both) + nn(w_gate[...], ds[blk])
 
     grads = (g_early, g_late)
-    cores = (core_early, core_late)
     rs_snd, rs_rcv = (rs_early, rs_late), (got_early, got_late)
     ag_snd, sums = (ag_early, ag_late), (sums_early, sums_late)
     others = pl.ds(0, planes - 1)
@@ -367,19 +364,36 @@
             halves = [grads[group][at, :, h * channels:(h + 1) * channels].reshape(groups, 8, channels) for h in range(2)]
             tiles.append(jnp.stack(swap(*halves), axis=1).reshape(planes, 8, channels))
         rs_snd[group][...] = jnp.concatenate(tiles, axis=1).astype(bf16)
-        send_rows(lambda to: rs_snd[group].at[to], rs_rcv[group], group, 0)
-        rs_rcv[group][plane] = rs_snd[group][plane]
-
-    def sum_cores(group):
-        wait(rs_rcv[group].at[others], g_rsem.at[group, 0])
-        cores[group][0] = jnp.sum(rs_rcv[group][...].astype(f32), axis=0) * (1.0 / n)
-        remote(cores[group].at[0], cores[group].at[1], g_ssem.at[group, 1], g_rsem.at[group, 1], other)
-
-    def share(group):
-        wait(cores[group].at[1], g_rsem.at[group, 1])
-        ag_snd[group][...] = (cores[group][0] + cores[group][1]).astype(bf16)
+        if group == EARLY:
+            send_rows(lambda to: rs_snd[group].at[to], rs_rcv[group], group, 0)
+            rs_rcv[group][plane] = rs_snd[group][plane]
+            return
+        for k in range(1, planes):
+            to, device = plane_peer(k)
+            for target in (device, device + 1 - 2 * core):
+                remote(rs_snd[group].at[to], rs_rcv[group].at[me], g_ssem.at[group, 0], g_rsem.at[group, 0], target)
+        remote(rs_snd[group].at[plane], rs_rcv[group].at[me], g_ssem.at[group, 0], g_rsem.at[group, 0], other)
+        rs_rcv[group][me] = rs_snd[group][plane]
+
+    def sum_cores():
+        wait(got_early.at[others], g_rsem.at[EARLY, 0])
+        core_early[0] = jnp.sum(got_early[...].astype(f32), axis=0) * (1.0 / n)
+        remote(core_early.at[0], core_early.at[1], g_ssem.at[EARLY, 1], g_rsem.at[EARLY, 1], other)
+
+    def share(group, rows):
+        ag_snd[group][...] = rows.astype(bf16)
         send_rows(lambda to: ag_snd[group], sums[group], group, 2)
         sums[group][plane] = ag_snd[group][...]
+
+    def share_early():
+        wait(core_early.at[1], g_rsem.at[EARLY, 1])
+        share(EARLY, core_early[0] + core_early[1])
+
+    every_other = pl.ds(0, devices - 1)
+
+    def share_late():
+        wait(got_late.at[every_other], g_rsem.at[LATE, 0])
+        share(LATE, jnp.sum(got_late[...].astype(f32), axis=0) * (1.0 / n))
 
     def last_sums(p):
         s_wait(DB, p)
@@ -406,8 +420,6 @@
         last_sums(p)
         last_grads(p)
 
-    s_sent(DB * chunks + chunks - 2)
-    s_sent(DB * chunks + chunks - 1)
     sum_planes(EARLY)
     last_sums(chunks - 2)
     last_grads(chunks - 2)
@@ -418,15 +430,18 @@
     for k in range(1, planes):
         remote(chain_snd, chain_rcv.at[plane], c_sem.at[0], c_sem.at[1], plane_peer(k)[1])
     chain_rcv[plane] = chain_snd[...]
-    sum_cores(EARLY)
-    share(EARLY)
-    sum_cores(LATE)
+    sum_cores()
+    share_early()
+    share_late()
     wait(chain_rcv.at[others], c_sem.at[1])
     chain_own[...] = jnp.sum(chain_rcv[...], axis=0) * (1.0 / n)
     remote(chain_own, chain_other, c_sem.at[2], c_sem.at[3], other)
-    share(LATE)
     wait(chain_other, c_sem.at[3])
     chain_out[...] = chain_own[...] + chain_other[...]
+
+    @pl.loop(0, 6 * chunks)
+    def _(i):
+        s_sent(i)
 
     @pl.loop(0, chunks)
     def _(p):
@@ -437,11 +452,12 @@
         wait(db_snd.at[c], d_ssem.at[c])
 
     for group in (EARLY, LATE):
-        wait(rs_snd[group].at[others], g_ssem.at[group, 0])
-        wait(cores[group].at[0], g_ssem.at[group, 1])
         wait(sums[group].at[others], g_ssem.at[group, 2])
         wait(sums[group].at[others], g_rsem.at[group, 2])
 
+    wait(rs_early.at[others], g_ssem.at[EARLY, 0])
+    wait(got_late.at[every_other], g_ssem.at[LATE, 0])
+    wait(core_early.at[0], g_ssem.at[EARLY, 1])
     wait(chain_rcv.at[others], c_sem.at[0])
     wait(chain_own, c_sem.at[2])
 
@@ -541,11 +557,10 @@
         vmem((1, channels), f32),
         vmem((1, channels), f32),
         vmem((2, 16, channels), f32),
-        vmem((2, 8, channels), f32),
         vmem((planes, 16, channels), bf16),
         vmem((planes, 8, channels), bf16),
         vmem((planes, 16, channels), bf16),
-        vmem((planes, 8, channels), bf16),
+        vmem((devices, 8, channels), bf16),
         vmem((16, channels), bf16),
         vmem((8, channels), bf16),
         sems((6 * chunks,)), sems((6, chunks)), sems((chunks,)), sems((chunks,)), sems((mine,)), sems((mine,)),

time: 65.9 us -> 65 us (0.986)
  Pallas kernels: 65.1 us -> 63.9 us
    pallas_call x1, Pallas kernels: 63.9 us -> 62.7 us  [on_device(): pl.pallas_call(functools.partial(kernel, devices), out_shape=(vmem(pair.s...]
where the time goes in v6:
time: 65 us; the launch traced here: 64.6 us
  Pallas kernels  63.9 us (98%)
    pallas_call x1, Pallas kernels, on_device(): pl.pallas_call(functools.partial(kernel, devices), out_shape=(vmem(pair.s...  62.7 us

profile of v6, /device:TPU:1, one launch (start us, length us, event | category | flops | bytes accessed | tf_op | source)
XLA Modules:
  0.0 64.6 jit_solution(10314279212501087638)
XLA Ops:
  0.6 62.7 %exchange.1 = (bf16[6,384,128]{2,1,0:T(8,128)(2,1)S(1)}, bf16[6,384,128]{2,1,0:T(8,128)(2,1)S(1)}, bf16[32,16,128]{2,1,0:T(8,128)(2,1)S(1)}, bf16[32,8,128]{2,1,0:T(8,128)(2,1)S(1)}, f32[1,128]{1,0:T(1,128)S(1)}) custom-call(bf16[6,384,128]{2,1,0:T(8,128)(2,1)} %pair_hbm.1, bf16[6,384,128]{2,1,0:T(8,128)(2,1)} %gout_hbm.1, s32[384]{0:T(512)} %pad_hbm.1, ...), custom_call_target="tpu_custom_call" | custom-call | flops 2000000000 | bytes 3000000 | tf_op jit(solution)/shard_map/exchange/pallas_call | solution.py:572
  63.4 1.2 %finish.1 = (bf16[6,384,128]{2,1,0:T(8,128)(2,1)}, bf16[6,384,128]{2,1,0:T(8,128)(2,1)}, f32[128,512]{1,0:T(8,128)}, f32[128,128]{1,0:T(8,128)}, f32[128,128]{1,0:T(8,128)}, /*index=5*/f32[1,128]{1,0:T(1,128)}) custom-call(bf16[6,384,128]{2,1,0:T(8,128)(2,1)S(1)} %get-tuple-element.17.update_v, bf16[6,384,128]{2,1,0:T(8,128)(2,1)S(1)} %get-tuple-element.18.gpair_v, ...), custom_call_target="tpu_custom_call" | custom-call | flops 1000000 | bytes 4000000 | tf_op jit(solution)/shard_map/finish/pallas_call | solution.py:588

commit v7 on v6

--- a/solution.py
+++ b/solution.py
@@ -161,9 +161,11 @@
         blk = p * chunks + kt
         both = nn(wt_in[first:first + 2 * channels, :], z[blk])
         sig, lin = sigmoid(both[:channels]), both[channels:]
-        sig_ref[blk] = sig
-        lin_ref[blk] = lin
-        put(u, p, kt, sig * lin * mask_of(p, kt))
+        masked = sig * mask_of(p, kt)
+        value = masked * lin
+        sig_ref[blk] = masked
+        lin_ref[blk] = value * (1.0 - sig)
+        put(u, p, kt, value)
 
     def turn_in(first):
         wt_in[first:first + channels, :] = w_in[:, first:first + channels].astype(f32).T.astype(bf16)
@@ -333,9 +335,8 @@
 
     def grad_project(u, p, kt, sig_ref, lin_ref):
         blk = p * chunks + kt
-        sig = sig_ref[blk]
-        grad = take(u, p, kt) * mask_of(p, kt) * sig
-        return jnp.concatenate([(grad * lin_ref[blk] * (1.0 - sig)).astype(bf16), grad.astype(bf16)], axis=0)
+        grad = take(u, p, kt)
+        return jnp.concatenate([(grad * lin_ref[blk]).astype(bf16), (grad * sig_ref[blk]).astype(bf16)], axis=0)
 
     @pl.loop(0, chunks)
     def _(p):

time: 65 us -> 64.9 us (level)
  no operation moved by 1% of the time
where the time goes in v7:
time: 64.9 us; the launch traced here: 64.7 us
  Pallas kernels  64.1 us (99%)
    pallas_call x1, Pallas kernels, on_device(): pl.pallas_call(functools.partial(kernel, devices), out_shape=(vmem(pair.s...  62.9 us

profile of v7, /device:TPU:1, one launch (start us, length us, event | category | flops | bytes accessed | tf_op | source)
XLA Modules:
  0.0 64.7 jit_solution(16299772398338602970)
XLA Ops:
  0.6 62.9 %exchange.1 = (bf16[6,384,128]{2,1,0:T(8,128)(2,1)S(1)}, bf16[6,384,128]{2,1,0:T(8,128)(2,1)S(1)}, bf16[32,16,128]{2,1,0:T(8,128)(2,1)S(1)}, bf16[32,8,128]{2,1,0:T(8,128)(2,1)S(1)}, f32[1,128]{1,0:T(1,128)S(1)}) custom-call(bf16[6,384,128]{2,1,0:T(8,128)(2,1)} %pair_hbm.1, bf16[6,384,128]{2,1,0:T(8,128)(2,1)} %gout_hbm.1, s32[384]{0:T(512)} %pad_hbm.1, ...), custom_call_target="tpu_custom_call" | custom-call | flops 2000000000 | bytes 3000000 | tf_op jit(solution)/shard_map/exchange/pallas_call | solution.py:573
  63.5 1.2 %finish.1 = (bf16[6,384,128]{2,1,0:T(8,128)(2,1)}, bf16[6,384,128]{2,1,0:T(8,128)(2,1)}, f32[128,512]{1,0:T(8,128)}, f32[128,128]{1,0:T(8,128)}, f32[128,128]{1,0:T(8,128)}, /*index=5*/f32[1,128]{1,0:T(1,128)}) custom-call(bf16[6,384,128]{2,1,0:T(8,128)(2,1)S(1)} %get-tuple-element.17.update_v, bf16[6,384,128]{2,1,0:T(8,128)(2,1)S(1)} %get-tuple-element.18.gpair_v, ...), custom_call_target="tpu_custom_call" | custom-call | flops 1000000 | bytes 4000000 | tf_op jit(solution)/shard_map/finish/pallas_call | solution.py:589
